TPU v7x, 32 devices: a whole 2x2x4 slice. The times are simulated.
32 devices in a mesh: clip: 2 (over x), row: 16 (over z, y, core).
Axes of the slice: x: 2, y: 2, z: 4, core: 2. Of those that a mesh axis runs over, the one named last changes fastest.
Arguments:
- source: bfloat16 [32768, 256], P(('clip', 'row')), parts along dimension 0, may hold values from -6 to 6
- near_blocks: bfloat16 [128, 16, 256, 256], P(('clip', 'row')), parts along dimension 0, may hold values from -0.125 to 0.125
- near_list: int32 [128, 16], P(('clip', 'row')), parts along dimension 0, may hold values from 0 to 63, as said below
- near_count: int32 [128], P(('clip', 'row')), parts along dimension 0, may hold values from 1 to 16
- col_basis: bfloat16 [128, 256, 128], P(('clip', 'row')), parts along dimension 0, may hold values from -0.375 to 0.375
- row_basis: bfloat16 [128, 256, 128], P(('clip', 'row')), parts along dimension 0, may hold values from -0.5 to 0.5
- transfer: bfloat16 [128, 128, 128], P(('clip', 'row')), parts along dimension 0, may hold values from -0.25 to 0.25
- far_list: int32 [128, 16], P(('clip', 'row')), parts along dimension 0, may hold values from 0 to 63, as said below
- far_coupling: bfloat16 [128, 16, 128, 128], P(('clip', 'row')), parts along dimension 0, may hold values from -0.125 to 0.125
- coarse_list: int32 [32, 8], P(('clip', 'row')), parts along dimension 0, may hold values from 0 to 15, as said below
- coarse_coupling: bfloat16 [32, 8, 128, 128], P(('clip', 'row')), parts along dimension 0, may hold values from -0.375 to 0.375
Outputs:
- product: bfloat16 [32768, 256], P(('clip', 'row')), parts along dimension 0
There are 2 independent parts, one for each index of `clip`. A program takes and returns all parts, laid end to end along the dimension named above; each array names one. Nothing has to cross between parts.
Inputs may be any that keep to these rules, and one draw needn't show every extreme that they name: near_list[i, 0] = i; the other entries lie within 4 leaves of i. far_list[i, f] lies in a coarse cluster one or two clusters away from that of leaf i. coarse_list[d, m] lies in the same aligned group of 16 coarse clusters as d, and its position in the group differs from that of d by three or more modulo 16.
All inputs are finite; a program needn't handle non-finite values.
Results may differ from a plain program's by a relative error of at most 0.0057.
Values may be sent and summed in bfloat16 or wider, within the bound.
No kernel may reach another device: no remote copies, remote signals or barrier semaphores. Data moves between devices by JAX's collectives and lax.ppermute only.
A program may use at most 128 MiB of HBM per device.

v0:
```python
import jax
import jax.numpy as jnp
from jax import lax
from jax.experimental import pallas as pl
from jax.experimental.pallas import tpu as pltpu
from jax.sharding import PartitionSpec as P

GROUP = 16
CHUNK = 4
MIB = 2**20

VMEM = pl.BlockSpec(memory_space=pltpu.VMEM)
SMEM = pl.BlockSpec(memory_space=pltpu.SMEM)
ANY = pl.BlockSpec(memory_space=pl.ANY)


def dot(a, b):
    return jnp.dot(a, b, preferred_element_type=jnp.float32)


def dot_t(a, b):
    return lax.dot_general(
        a, b, (((0,), (0,)), ((), ())), preferred_element_type=jnp.float32
    )


def rows_at(index, rows):
    return pl.ds(pl.multiple_of(index * rows, rows), rows)


def coef_kernel(source_ref, col_ref, share_ref, coef_ref):
    leaves, rows, rank = col_ref.shape
    for leaf in range(leaves):
        panel = source_ref[pl.ds(leaf * rows, rows), :]
        share_ref[pl.ds(leaf * rows, rows), :] = panel
        coef = dot_t(col_ref[leaf], panel).astype(jnp.bfloat16)
        coef_ref[pl.ds(leaf * rank, rank), :] = coef
        share_ref[pl.ds(leaves * rows + leaf * rank, rank), :] = coef


def parent_kernel(coef_ref, transfer_ref, parent_ref):
    leaves, rank, _ = transfer_ref.shape
    total = None
    for leaf in range(leaves):
        term = dot_t(transfer_ref[leaf], coef_ref[pl.ds(leaf * rank, rank), :])
        total = term if total is None else total + term
    parent_ref[...] = total.astype(jnp.bfloat16)


def join_kernel(*refs):
    *pieces, _, out_ref = refs
    at = 0
    for ref in pieces:
        out_ref[pl.ds(at, ref.shape[0]), :] = ref[...]
        at += ref.shape[0]


def pick_kernel(level_ref, layer_ref, out_ref):
    corner = lax.axis_index("row") & 3
    level = (corner == 0) | (corner == 3)
    out_ref[...] = jnp.where(level, level_ref[...], layer_ref[...])


def hand_kernel(in_ref, *refs):
    out_ref = refs[-1]
    out_ref[...] = in_ref[pl.ds(0, out_ref.shape[0]), :]


def pick_slots(index_ref, blocks_hbm, blocks, sems, order_ref, low, high):
    leaves, slots, rows, _ = blocks.shape

    def picker(leaf):
        def step(slot, found):
            panel = index_ref[leaf, slot]
            kept = (panel >= low) & (panel < high)

            @pl.when(kept)
            def _():
                order_ref[leaf, found] = panel - low
                pltpu.make_async_copy(
                    blocks_hbm.at[leaf, slot], blocks.at[leaf, found], sems.at[leaf, found]
                ).start()

            return found + kept.astype(jnp.int32)

        return step

    found = [lax.fori_loop(0, slots, picker(leaf), 0) for leaf in range(leaves)]
    for leaf in range(leaves):
        for pad in range(CHUNK):
            order_ref[leaf, found[leaf] + pad] = high - low
    return found


def add_slots(total_ref, blocks_hbm, blocks, sems, order_ref, found, panels):
    leaves, slots, rows, _ = blocks.shape
    for leaf in range(leaves):
        count = found[leaf]

        def term(n):
            block = blocks[leaf, jnp.where(n < count, n, 0)]
            return dot(block, panels[rows_at(order_ref[leaf, n], rows), :])

        for first in range(0, slots, CHUNK):
            @pl.when(first < count)
            def _():
                for n in range(first, first + CHUNK):
                    @pl.when(n < count)
                    def _():
                        pltpu.make_async_copy(
                            blocks_hbm.at[leaf, 0], blocks.at[leaf, n], sems.at[leaf, n]
                        ).wait()
                even = term(first) + term(first + 2)
                odd = term(first + 1) + term(first + 3)
                total_ref[leaf] = total_ref[leaf] + (even + odd)


def near_kernel(
    index_ref, blocks_hbm, own_ref, share_ref,
    near_ref,
    blocks, panels, order, block_sems, panel_sems,
):
    leaves, _, rows, _ = blocks.shape
    size = leaves * rows
    pairs = [
        pltpu.make_async_copy(
            ref.at[pl.ds(0, size)], panels.at[pl.ds(which * size, size)], panel_sems.at[which]
        )
        for which, ref in enumerate((own_ref, share_ref))
    ]
    for copy in pairs:
        copy.start()
    found = pick_slots(index_ref, blocks_hbm, blocks, block_sems, order, 0, 2 * leaves)
    near_ref[...] = jnp.zeros(near_ref.shape, near_ref.dtype)
    panels[pl.ds(2 * size, rows), :] = jnp.zeros((rows, panels.shape[1]), panels.dtype)
    for copy in pairs:
        copy.wait()
    add_slots(near_ref, blocks_hbm, blocks, block_sems, order, found, panels)


def across_kernel(
    index_ref, blocks_hbm, near_ref, across_ref,
    total_ref,
    blocks, panels, order, block_sems, panel_sems,
):
    leaves, _, rows, _ = blocks.shape
    size = leaves * rows
    copy = pltpu.make_async_copy(across_ref, panels.at[pl.ds(0, size)], panel_sems.at[0])
    copy.start()
    found = pick_slots(
        index_ref, blocks_hbm, blocks, block_sems, order, 2 * leaves, 3 * leaves
    )
    total_ref[...] = near_ref[...]
    panels[pl.ds(size, rows), :] = jnp.zeros((rows, panels.shape[1]), panels.dtype)
    copy.wait()
    add_slots(total_ref, blocks_hbm, blocks, block_sems, order, found, panels)


def far_kernel(
    list_ref, coupling_ref, level_ref, layer_ref, share_ref, passed_ref,
    far_ref,
    coefs, sems,
):
    leaves, slots, rank, _ = coupling_ref.shape
    size = leaves * rank
    place = lax.axis_index("row")
    beyond = jnp.where((place & 2) == 0, place - 2, place + 2)
    copies = [
        pltpu.make_async_copy(
            ref.at[pl.ds(ref.shape[0] - size, size)], coefs.at[pl.ds(n * size, size)], sems.at[n]
        )
        for n, ref in enumerate((level_ref, layer_ref, share_ref, passed_ref))
    ]
    for copy in copies:
        copy.start()
    for copy in copies:
        copy.wait()

    def panel_of(leaf, slot):
        column = list_ref[leaf, slot]
        cluster = lax.div(column, leaves)
        which = jnp.where(
            cluster == (place ^ 2), 0,
            jnp.where(cluster == beyond, 1, jnp.where(cluster == (place ^ 1), 2, 3)),
        )
        return coefs[rows_at(which * leaves + column - cluster * leaves, rank), :]

    for leaf in range(leaves):
        total = None
        for slot in range(0, slots, 2):
            both = jnp.concatenate([coupling_ref[leaf, slot], coupling_ref[leaf, slot + 1]], axis=1)
            panels = jnp.concatenate([panel_of(leaf, slot), panel_of(leaf, slot + 1)], axis=0)
            term = dot(both, panels)
            total = term if total is None else total + term
        far_ref[pl.ds(leaf * rank, rank), :] = total


def down_kernel(
    list_ref, transfer_ref, coupling_ref, row_ref, near_ref, far_ref,
    column_ref, beside_ref, their_column_ref, their_beside_ref,
    out_ref,
):
    leaves, rows, rank = row_ref.shape
    local = lax.axis_index("row") & (GROUP - 1)

    def panel_of(slot):
        flip = (list_ref[0, slot] & (GROUP - 1)) ^ local
        where = rows_at(flip >> 2, rank)
        mine = jnp.where((flip & 2) == 0, column_ref[where, :], beside_ref[where, :])
        theirs = jnp.where((flip & 2) == 0, their_column_ref[where, :], their_beside_ref[where, :])
        return jnp.where((flip & 1) == 0, mine, theirs)

    terms = []
    for slot in range(0, list_ref.shape[1], 2):
        both = jnp.concatenate([coupling_ref[0, slot], coupling_ref[0, slot + 1]], axis=1)
        terms.append(dot(both, jnp.concatenate([panel_of(slot), panel_of(slot + 1)], axis=0)))
    while len(terms) > 1:
        terms = [first + second for first, second in zip(terms[::2], terms[1::2])]
    high = terms[0].astype(jnp.bfloat16)
    low = (terms[0] - high.astype(jnp.float32)).astype(jnp.bfloat16)
    matrix = transfer_ref[...].reshape(leaves * rank, rank)
    spread = dot(
        jnp.concatenate([matrix, matrix], axis=1), jnp.concatenate([high, low], axis=0)
    )
    down = (far_ref[...] + spread).astype(jnp.bfloat16)
    for leaf in range(leaves):
        result = near_ref[leaf] + dot(row_ref[leaf], down[leaf * rank:(leaf + 1) * rank])
        out_ref[pl.ds(leaf * rows, rows), :] = result.astype(jnp.bfloat16)


def call(kernel, name, outs, specs, args, scratch=(), flops=0, moved=0, limit=4):
    many = isinstance(outs, tuple)
    return pl.pallas_call(
        kernel,
        out_shape=outs,
        in_specs=specs,
        out_specs=(VMEM,) * len(outs) if many else VMEM,
        scratch_shapes=list(scratch),
        cost_estimate=pl.CostEstimate(flops=flops, bytes_accessed=moved, transcendentals=0),
        compiler_params=pltpu.CompilerParams(vmem_limit_bytes=limit * MIB),
        name=name,
    )(*args)


def body(
    source,
    near_blocks,
    near_list,
    near_count,
    col_basis,
    row_basis,
    transfer,
    far_list,
    far_coupling,
    coarse_list,
    coarse_coupling,
):
    leaves, slots, rows, _ = near_blocks.shape
    rank = col_basis.shape[2]
    width = source.shape[1]
    count = lax.axis_size("row")
    far_slots = far_coupling.shape[1]

    def send(value, target):
        pairs = [(d, target(d)) for d in range(count) if 0 <= target(d) < count]
        return lax.ppermute(value, "row", pairs)

    def panel(blocks, dtype=jnp.bfloat16):
        return jax.ShapeDtypeStruct((blocks * rank, width), dtype)

    share, coef = call(
        coef_kernel, "coef",
        (jax.ShapeDtypeStruct((leaves * (rows + rank), width), jnp.bfloat16), panel(leaves)),
        [VMEM] * 2, (source, col_basis), flops=2 * leaves * rank * width * rows,
        moved=2 * leaves * rows * (width + rank), limit=8,
    )
    parent = call(parent_kernel, "parent", panel(1), [VMEM] * 2, (coef, transfer))
    layers = [send(parent, lambda d, bit=bit: d ^ bit) for bit in (4, 8, 12)]
    share_other = send(share, lambda d: d ^ 1)
    level = send(coef, lambda d: d ^ 2)
    panels = call(
        hand_kernel, "panels", jax.ShapeDtypeStruct(source.shape, jnp.bfloat16), [VMEM] + [ANY] * 1,
        (share, share_other),
    )
    across = send(panels, lambda d: d + 1 if d & 1 else d - 1)

    place = lax.axis_index("row")
    live = lax.broadcasted_iota(jnp.int32, (leaves, slots), 1) < near_count[:, None]
    which = jnp.minimum((near_list // leaves) ^ place, 2)
    index = jnp.where(live, which * leaves + near_list % leaves, 3 * leaves)
    def slots_scratch(panels):
        return [
            pltpu.VMEM(near_blocks.shape, jnp.bfloat16),
            pltpu.VMEM((panels * rows, width), jnp.bfloat16),
            pltpu.SMEM((leaves, slots + CHUNK), jnp.int32),
            pltpu.SemaphoreType.DMA((leaves, slots)),
            pltpu.SemaphoreType.DMA((2,)),
        ]

    shape = jax.ShapeDtypeStruct((leaves, rows, width), jnp.float32)
    near = call(
        near_kernel, "near", shape, [SMEM] + [ANY] * 3,
        (index, near_blocks, share, share_other),
        scratch=slots_scratch(2 * leaves + 1), flops=10**9, limit=48,
    )
    layer = send(level, lambda d: d - 4 if d & 2 else d + 4)
    column = call(join_kernel, "column", panel(GROUP // 4), [VMEM] * 4 + [ANY],
        (parent, *layers, near))
    beside = send(column, lambda d: d ^ 2)
    their_column = send(column, lambda d: d ^ 1)
    near = call(
        across_kernel, "across", shape, [SMEM, ANY, VMEM, ANY],
        (index, near_blocks, near, across),
        scratch=slots_scratch(leaves + 1), flops=0, limit=48,
    )
    picked_coef = call(
        pick_kernel, "pick", panel(leaves), [VMEM] * 2, (level, layer)
    )
    passed = send(picked_coef, lambda d: d ^ 1)
    far = call(
        far_kernel, "far", panel(leaves, jnp.float32), [SMEM, VMEM] + [ANY] * 4,
        (far_list, far_coupling, level, layer, share_other, passed),
        scratch=[
            pltpu.VMEM((4 * leaves * rank, width), jnp.bfloat16),
            pltpu.SemaphoreType.DMA((4,)),
        ],
        flops=2 * leaves * far_slots * rank * rank * width,
        moved=2 * leaves * far_slots * rank * rank, limit=10,
    )
    handed = call(hand_kernel, "hand", panel(GROUP // 4), [VMEM, ANY], (beside, near))
    their_beside = send(handed, lambda d: d ^ 1)
    return call(
        down_kernel, "down", jax.ShapeDtypeStruct(source.shape, jnp.bfloat16),
        [SMEM] + [VMEM] * 9,
        (
            coarse_list, transfer, coarse_coupling, row_basis, near, far,
            column, handed, their_column, their_beside,
        ),
        flops=8 * leaves * rank * rank * width,
        moved=4 * leaves * rows * width, limit=8,
    )


def solution(mesh):
    placed = (
        P(("clip", "row"), None),
        P(("clip", "row"), None, None, None),
        P(("clip", "row"), None),
        P(("clip", "row")),
        P(("clip", "row"), None, None),
        P(("clip", "row"), None, None),
        P(("clip", "row"), None, None),
        P(("clip", "row"), None),
        P(("clip", "row"), None, None, None),
        P(("clip", "row"), None),
        P(("clip", "row"), None, None, None),
    )
    return jax.shard_map(
        body, mesh=mesh, in_specs=placed, out_specs=P(("clip", "row"), None), check_vma=False
    )
```

profile of v0, /device:TPU:27, one launch (start us, length us, event | category | flops | bytes accessed | tf_op | source)
XLA Modules:
  0.0 35.3 jit_solution(12057812268281736730)
XLA Ops:
  0.0 0.0 copy-start.3
  0.0 1.0 %copy-done.3 = bf16[1024,256]{1,0:T(8,128)(2,1)S(1)} copy-done((bf16[1024,256]{1,0:T(8,128)(2,1)S(1)}, bf16[1024,256]{1,0:T(8,128)(2,1)}, u32[]{:S(2)}) %copy-start.3) | copy-done | bytes 524312
  1.0 0.0 copy-start.4
  1.0 0.9 %copy-done.4 = bf16[4,256,128]{2,1,0:T(8,128)(2,1)S(1)} copy-done((bf16[4,256,128]{2,1,0:T(8,128)(2,1)S(1)}, bf16[4,256,128]{2,1,0:T(8,128)(2,1)}, u32[]{:S(2)}) %copy-start.4) | copy-done | bytes 262168
  2.0 0.3 coef.1
  2.3 0.7 %collective-permute-start = (bf16[1536,256]{1,0:T(8,128)(2,1)S(1)}, bf16[1536,256]{1,0:T(8,128)(2,1)S(1)}, u32[]{:S(2)}, u32[]{:S(2)}) collective-permute-start(bf16[1536,256]{1,0:T(8,128)(2,1)S(1)} %get-tuple-element.7.own_ref.in_ref), channel_id=1, source_target_pairs={{0,1},{1,0},{2,3},{3,2},{4,5},{5,4},{6,7},{7,6},{8,9},{9,8},{10,11... | collective-permute-start | bytes 2359304 | tf_op jit(solution)/shard_map/ppermute | solution.py:266
  3.0 1.3 %collective-permute-start.2 = (bf16[512,256]{1,0:T(8,128)(2,1)S(1)}, bf16[512,256]{1,0:T(8,128)(2,1)S(1)}, u32[]{:S(2)}, u32[]{:S(2)}) collective-permute-start(bf16[512,256]{1,0:T(8,128)(2,1)S(1)} %get-tuple-element.8.coef_ref), channel_id=1, source_target_pairs={{0,2},{1,3},{2,0},{3,1},{4,6},{5,7},{6,4},{7,5},{8,10},{9,11},{10,... | collective-permute-start | bytes 786440 | tf_op jit(solution)/shard_map/ppermute | solution.py:266
  4.3 0.0 copy-start.1
  4.3 0.9 %copy-done.1 = bf16[4,128,128]{2,1,0:T(8,128)(2,1)S(1)} copy-done((bf16[4,128,128]{2,1,0:T(8,128)(2,1)S(1)}, bf16[4,128,128]{2,1,0:T(8,128)(2,1)}, u32[]{:S(2)}) %copy-start.1) | copy-done | bytes 131096
  5.2 0.3 parent.1.refs_0_
  5.4 0.1 collective-permute-start.7
  5.5 1.3 %collective-permute-start.6 = (bf16[128,256]{1,0:T(8,128)(2,1)S(1)}, bf16[128,256]{1,0:T(8,128)(2,1)S(1)}, u32[]{:S(2)}, u32[]{:S(2)}) collective-permute-start(bf16[128,256]{1,0:T(8,128)(2,1)S(1)} %parent.1.refs_0_), channel_id=1, source_target_pairs={{0,8},{1,9},{2,10},{3,11},{4,12},{5,13},{6,14},{7,15},{8,0},{9,1},... | collective-permute-start | bytes 196616 | tf_op jit(solution)/shard_map/ppermute | solution.py:266
  6.8 2.2 %collective-permute-start.5 = (bf16[128,256]{1,0:T(8,128)(2,1)S(1)}, bf16[128,256]{1,0:T(8,128)(2,1)S(1)}, u32[]{:S(2)}, u32[]{:S(2)}) collective-permute-start(bf16[128,256]{1,0:T(8,128)(2,1)S(1)} %parent.1.refs_0_), channel_id=1, source_target_pairs={{0,4},{1,5},{2,6},{3,7},{4,0},{5,1},{6,2},{7,3},{8,12},{9,13},{10,... | collective-permute-start | bytes 196616 | tf_op jit(solution)/shard_map/ppermute | solution.py:266
  9.0 0.0 collective-permute-done.share_ref.refs_0_
  9.1 3.2 %collective-permute-start.1 = (bf16[1024,256]{1,0:T(8,128)(2,1)S(1)}, bf16[1024,256]{1,0:T(8,128)(2,1)S(1)}, u32[]{:S(2)}, u32[]{:S(2)}) collective-permute-start(bf16[1024,256]{1,0:T(8,128)(2,1)S(1)} %panels.1), channel_id=1, source_target_pairs={{1,2},{2,1},{3,4},{4,3},{5,6},{6,5},{7,8},{8,7},{9,10},{10,9},{11,... | collective-permute-start | bytes 1572872 | tf_op jit(solution)/shard_map/ppermute | solution.py:266
  12.3 0.8 %fusion.4.index_ref = s32[4,16]{1,0:T(4,128)S(1)} fusion(s32[4,16]{1,0:T(4,128)} %param.13, s32[]{:T(128)S(6)} %axis_index.12, s32[4]{0:T(128)} %param.14), kind=kLoop, calls=%fused_computation.9 | loop fusion | flops 1600 | bytes 532 | tf_op jit(solution)/shard_map/jit(_where)/select_n | solution.py:290
  13.1 0.0 collective-permute-done.2.level_ref
  13.1 1.3 %collective-permute-start.3 = (bf16[512,256]{1,0:T(8,128)(2,1)S(1)}, bf16[512,256]{1,0:T(8,128)(2,1)S(1)}, u32[]{:S(2)}, u32[]{:S(2)}) collective-permute-start(bf16[512,256]{1,0:T(8,128)(2,1)S(1)} %collective-permute-done.2.level_ref), channel_id=1, source_target_pairs={{0,4},{1,5},{4,8},{5,9},{6,2},{7,3},{8,12},{9,13},{10,6},{11,7},{1... | collective-permute-start | bytes 786440 | tf_op jit(solution)/shard_map/ppermute | solution.py:266
  14.3 4.9 %near.1.near_ref.refs_4_ = f32[4,256,256]{2,1,0:T(8,128)S(1)} custom-call(s32[4,16]{1,0:T(4,128)S(1)} %fusion.4.index_ref, bf16[4,16,256,256]{3,2,1,0:T(8,128)(2,1)} %blocks_hbm.3, bf16[1536,256]{1,0:T(8,128)(2,1)S(1)} %get-tuple-element.7.own_ref.in_ref, bf16[1536,256]{1,0:T(8,128)(2,1)S(1)} %collective-permute-done.share_ref.refs_0_), custom_call_target="tpu_custom_call" | custom-call | flops 1000000000 | tf_op jit(solution)/shard_map/near/pallas_call | solution.py:233
  19.2 0.0 copy-start
  19.2 0.0 copy-start.7
  19.2 0.0 collective-permute-done.7.refs_3_
  19.2 0.0 collective-permute-done.6.refs_2_
  19.3 0.0 collective-permute-done.5.refs_1_
  19.3 2.7 %collective-permute-start.8 = (bf16[512,256]{1,0:T(8,128)(2,1)S(1)}, bf16[512,256]{1,0:T(8,128)(2,1)S(1)}, u32[]{:S(2)}, u32[]{:S(2)}) collective-permute-start(bf16[512,256]{1,0:T(8,128)(2,1)S(1)} %column.1.column_ref), channel_id=1, source_target_pairs={{0,2},{1,3},{2,0},{3,1},{4,6},{5,7},{6,4},{7,5},{8,10},{9,11},{10,... | collective-permute-start | bytes 786440 | tf_op jit(solution)/shard_map/ppermute | solution.py:266
  22.0 1.0 %collective-permute-done.3.layer_ref = bf16[512,256]{1,0:T(8,128)(2,1)S(1)} collective-permute-done((bf16[512,256]{1,0:T(8,128)(2,1)S(1)}, bf16[512,256]{1,0:T(8,128)(2,1)S(1)}, u32[]{:S(2)}, u32[]{:S(2)}) %collective-permute-start.3) | collective-permute-done | bytes 262176 | tf_op jit(solution)/shard_map/ppermute | solution.py:266
  23.0 0.0 copy-start.2
  23.0 0.0 copy-start.5
  23.1 0.0 copy-start.6
  23.1 0.0 copy-start.8
  23.1 0.7 %collective-permute-start.4 = (bf16[512,256]{1,0:T(8,128)(2,1)S(1)}, bf16[512,256]{1,0:T(8,128)(2,1)S(1)}, u32[]{:S(2)}, u32[]{:S(2)}) collective-permute-start(bf16[512,256]{1,0:T(8,128)(2,1)S(1)} %pick.1), channel_id=1, source_target_pairs={{0,1},{1,0},{2,3},{3,2},{4,5},{5,4},{6,7},{7,6},{8,9},{9,8},{10,11... | collective-permute-start | bytes 786440 | tf_op jit(solution)/shard_map/ppermute | solution.py:266
  23.8 0.1 collective-permute-start.9
  23.9 3.5 %collective-permute-done.1.across_ref = bf16[1024,256]{1,0:T(8,128)(2,1)S(1)} collective-permute-done((bf16[1024,256]{1,0:T(8,128)(2,1)S(1)}, bf16[1024,256]{1,0:T(8,128)(2,1)S(1)}, u32[]{:S(2)}, u32[]{:S(2)}) %collective-permute-start.1) | collective-permute-done | bytes 524320 | tf_op jit(solution)/shard_map/ppermute | solution.py:266
  27.4 3.2 %across.1.refs_0_.near_ref = f32[4,256,256]{2,1,0:T(8,128)S(1)} custom-call(s32[4,16]{1,0:T(4,128)S(1)} %fusion.4.index_ref, bf16[4,16,256,256]{3,2,1,0:T(8,128)(2,1)} %blocks_hbm.3, f32[4,256,256]{2,1,0:T(8,128)S(1)} %near.1.near_ref.refs_4_, bf16[1024,256]{1,0:T(8,128)(2,1)S(1)} %collective-permute-done.1.across_ref), custom_call_target="tpu_custom_call" | custom-call | tf_op jit(solution)/shard_map/across/pallas_call | solution.py:233
  30.6 0.0 collective-permute-done.8.in_ref
  30.7 0.9 %collective-permute-start.10 = (bf16[512,256]{1,0:T(8,128)(2,1)S(1)}, bf16[512,256]{1,0:T(8,128)(2,1)S(1)}, u32[]{:S(2)}, u32[]{:S(2)}) collective-permute-start(bf16[512,256]{1,0:T(8,128)(2,1)S(1)} %hand.1.beside_ref), channel_id=1, source_target_pairs={{0,1},{1,0},{2,3},{3,2},{4,5},{5,4},{6,7},{7,6},{8,9},{9,8},{10,11... | collective-permute-start | bytes 786440 | tf_op jit(solution)/shard_map/ppermute | solution.py:266
  31.6 0.0 collective-permute-done.4.passed_ref
  31.6 0.0 copy-done
  31.6 0.0 copy-done.7
  31.6 1.5 %far.1.far_ref = f32[512,256]{1,0:T(8,128)S(1)} custom-call(s32[4,16]{1,0:T(4,128)S(1)} %copy-done.7, bf16[4,16,128,128]{3,2,1,0:T(8,128)(2,1)S(1)} %copy-done, bf16[512,256]{1,0:T(8,128)(2,1)S(1)} %collective-permute-done.2.level_ref, bf16[512,256]{1,0:T(8,128)(2,1)S(1)} %collective-permute-done.3.layer_ref, ...), custom_call_target="tpu_custom_call" | custom-call | flops 536870912 | bytes 2097152 | tf_op jit(solution)/shard_map/far/pallas_call | solution.py:233
  33.1 0.0 collective-permute-done.9.their_column_ref
  33.1 0.0 collective-permute-done.10.their_beside_ref
  33.1 0.0 copy-done.2
  33.1 0.0 copy-done.5
  33.1 0.0 copy-done.6
  33.1 0.0 copy-done.8
  33.2 2.1 %down.1 = bf16[1024,256]{1,0:T(8,128)(2,1)} custom-call(s32[1,8]{1,0:T(1,128)S(1)} %copy-done.8, bf16[4,128,128]{2,1,0:T(8,128)(2,1)S(1)} %copy-done.2, bf16[1,8,128,128]{3,2,1,0:T(8,128)(2,1)S(1)} %copy-done.5, bf16[4,256,128]{2,1,0:T(8,128)(2,1)S(1)} %copy-done.6, f32[4,256,256]{2,1,0:T(8,128)S(1)} %across.1.refs_0_.near_ref, f32[512,256]{1,0:T(8,128)S(1)} %far.1.far_ref, ...), custom_call_target="tpu_custom_call" | custom-call | flops 134217728 | bytes 1048576 | tf_op jit(solution)/shard_map/down/pallas_call | solution.py:233
  (4 shorter events, 0.1 us)
Async XLA Ops:
  0.0 1.0 %copy-start.3 = (bf16[1024,256]{1,0:T(8,128)(2,1)S(1)}, bf16[1024,256]{1,0:T(8,128)(2,1)}, u32[]{:S(2)}) copy-start(bf16[1024,256]{1,0:T(8,128)(2,1)} %source_ref.1) | copy-start | bytes 1572868
  1.0 0.9 %copy-start.4 = (bf16[4,256,128]{2,1,0:T(8,128)(2,1)S(1)}, bf16[4,256,128]{2,1,0:T(8,128)(2,1)}, u32[]{:S(2)}) copy-start(bf16[4,256,128]{2,1,0:T(8,128)(2,1)} %col_ref.1) | copy-start | bytes 786436
  2.3 6.8 %collective-permute-start = (bf16[1536,256]{1,0:T(8,128)(2,1)S(1)}, bf16[1536,256]{1,0:T(8,128)(2,1)S(1)}, u32[]{:S(2)}, u32[]{:S(2)}) collective-permute-start(bf16[1536,256]{1,0:T(8,128)(2,1)S(1)} %get-tuple-element.7.own_ref.in_ref), channel_id=1, source_target_pairs={{0,1},{1,0},{2,3},{3,2},{4,5},{5,4},{6,7},{7,6},{8,9},{9,8},{10,11... | collective-permute-start | bytes 2359304 | tf_op jit(solution)/shard_map/ppermute | solution.py:266
  3.0 10.0 %collective-permute-start.2 = (bf16[512,256]{1,0:T(8,128)(2,1)S(1)}, bf16[512,256]{1,0:T(8,128)(2,1)S(1)}, u32[]{:S(2)}, u32[]{:S(2)}) collective-permute-start(bf16[512,256]{1,0:T(8,128)(2,1)S(1)} %get-tuple-element.8.coef_ref), channel_id=1, source_target_pairs={{0,2},{1,3},{2,0},{3,1},{4,6},{5,7},{6,4},{7,5},{8,10},{9,11},{10,... | collective-permute-start | bytes 786440 | tf_op jit(solution)/shard_map/ppermute | solution.py:266
  4.3 0.9 %copy-start.1 = (bf16[4,128,128]{2,1,0:T(8,128)(2,1)S(1)}, bf16[4,128,128]{2,1,0:T(8,128)(2,1)}, u32[]{:S(2)}) copy-start(bf16[4,128,128]{2,1,0:T(8,128)(2,1)} %transfer_ref.3) | copy-start | bytes 393220
  5.4 13.8 %collective-permute-start.7 = (bf16[128,256]{1,0:T(8,128)(2,1)S(1)}, bf16[128,256]{1,0:T(8,128)(2,1)S(1)}, u32[]{:S(2)}, u32[]{:S(2)}) collective-permute-start(bf16[128,256]{1,0:T(8,128)(2,1)S(1)} %parent.1.refs_0_), channel_id=1, source_target_pairs={{0,12},{1,13},{2,14},{3,15},{4,8},{5,9},{6,10},{7,11},{8,4},{9,5},... | collective-permute-start | bytes 196616 | tf_op jit(solution)/shard_map/ppermute | solution.py:266
  5.5 13.7 %collective-permute-start.6 = (bf16[128,256]{1,0:T(8,128)(2,1)S(1)}, bf16[128,256]{1,0:T(8,128)(2,1)S(1)}, u32[]{:S(2)}, u32[]{:S(2)}) collective-permute-start(bf16[128,256]{1,0:T(8,128)(2,1)S(1)} %parent.1.refs_0_), channel_id=1, source_target_pairs={{0,8},{1,9},{2,10},{3,11},{4,12},{5,13},{6,14},{7,15},{8,0},{9,1},... | collective-permute-start | bytes 196616 | tf_op jit(solution)/shard_map/ppermute | solution.py:266
  6.8 12.4 %collective-permute-start.5 = (bf16[128,256]{1,0:T(8,128)(2,1)S(1)}, bf16[128,256]{1,0:T(8,128)(2,1)S(1)}, u32[]{:S(2)}, u32[]{:S(2)}) collective-permute-start(bf16[128,256]{1,0:T(8,128)(2,1)S(1)} %parent.1.refs_0_), channel_id=1, source_target_pairs={{0,4},{1,5},{2,6},{3,7},{4,0},{5,1},{6,2},{7,3},{8,12},{9,13},{10,... | collective-permute-start | bytes 196616 | tf_op jit(solution)/shard_map/ppermute | solution.py:266
  9.1 18.3 %collective-permute-start.1 = (bf16[1024,256]{1,0:T(8,128)(2,1)S(1)}, bf16[1024,256]{1,0:T(8,128)(2,1)S(1)}, u32[]{:S(2)}, u32[]{:S(2)}) collective-permute-start(bf16[1024,256]{1,0:T(8,128)(2,1)S(1)} %panels.1), channel_id=1, source_target_pairs={{1,2},{2,1},{3,4},{4,3},{5,6},{6,5},{7,8},{8,7},{9,10},{10,9},{11,... | collective-permute-start | bytes 1572872 | tf_op jit(solution)/shard_map/ppermute | solution.py:266
  13.1 9.9 %collective-permute-start.3 = (bf16[512,256]{1,0:T(8,128)(2,1)S(1)}, bf16[512,256]{1,0:T(8,128)(2,1)S(1)}, u32[]{:S(2)}, u32[]{:S(2)}) collective-permute-start(bf16[512,256]{1,0:T(8,128)(2,1)S(1)} %collective-permute-done.2.level_ref), channel_id=1, source_target_pairs={{0,4},{1,5},{4,8},{5,9},{6,2},{7,3},{8,12},{9,13},{10,6},{11,7},{1... | collective-permute-start | bytes 786440 | tf_op jit(solution)/shard_map/ppermute | solution.py:266
  19.2 12.4 %copy-start = (bf16[4,16,128,128]{3,2,1,0:T(8,128)(2,1)S(1)}, bf16[4,16,128,128]{3,2,1,0:T(8,128)(2,1)}, u32[]{:S(2)}) copy-start(bf16[4,16,128,128]{3,2,1,0:T(8,128)(2,1)} %coupling_ref.2) | copy-start | bytes 6291460
  19.2 12.4 %copy-start.7 = (s32[4,16]{1,0:T(4,128)S(1)}, s32[4,16]{1,0:T(4,128)}, u32[]{:S(2)}) copy-start(s32[4,16]{1,0:T(4,128)} %list_ref.2) | copy-start | bytes 772
  19.3 11.4 %collective-permute-start.8 = (bf16[512,256]{1,0:T(8,128)(2,1)S(1)}, bf16[512,256]{1,0:T(8,128)(2,1)S(1)}, u32[]{:S(2)}, u32[]{:S(2)}) collective-permute-start(bf16[512,256]{1,0:T(8,128)(2,1)S(1)} %column.1.column_ref), channel_id=1, source_target_pairs={{0,2},{1,3},{2,0},{3,1},{4,6},{5,7},{6,4},{7,5},{8,10},{9,11},{10,... | collective-permute-start | bytes 786440 | tf_op jit(solution)/shard_map/ppermute | solution.py:266
  23.0 10.1 %copy-start.2 = (bf16[4,128,128]{2,1,0:T(8,128)(2,1)S(1)}, bf16[4,128,128]{2,1,0:T(8,128)(2,1)}, u32[]{:S(2)}) copy-start(bf16[4,128,128]{2,1,0:T(8,128)(2,1)} %transfer_ref.3) | copy-start | bytes 393220
  23.0 10.1 %copy-start.5 = (bf16[1,8,128,128]{3,2,1,0:T(8,128)(2,1)S(1)}, bf16[1,8,128,128]{3,2,1,0:T(8,128)(2,1)}, u32[]{:S(2)}) copy-start(bf16[1,8,128,128]{3,2,1,0:T(8,128)(2,1)} %coupling_ref.3) | copy-start | bytes 786436
  23.1 10.1 %copy-start.6 = (bf16[4,256,128]{2,1,0:T(8,128)(2,1)S(1)}, bf16[4,256,128]{2,1,0:T(8,128)(2,1)}, u32[]{:S(2)}) copy-start(bf16[4,256,128]{2,1,0:T(8,128)(2,1)} %row_ref.1) | copy-start | bytes 786436
  23.1 10.1 %copy-start.8 = (s32[1,8]{1,0:T(1,128)S(1)}, s32[1,8]{1,0:T(1,128)}, u32[]{:S(2)}) copy-start(s32[1,8]{1,0:T(1,128)} %list_ref.3) | copy-start | bytes 100
  23.1 8.5 %collective-permute-start.4 = (bf16[512,256]{1,0:T(8,128)(2,1)S(1)}, bf16[512,256]{1,0:T(8,128)(2,1)S(1)}, u32[]{:S(2)}, u32[]{:S(2)}) collective-permute-start(bf16[512,256]{1,0:T(8,128)(2,1)S(1)} %pick.1), channel_id=1, source_target_pairs={{0,1},{1,0},{2,3},{3,2},{4,5},{5,4},{6,7},{7,6},{8,9},{9,8},{10,11... | collective-permute-start | bytes 786440 | tf_op jit(solution)/shard_map/ppermute | solution.py:266
  23.8 9.3 %collective-permute-start.9 = (bf16[512,256]{1,0:T(8,128)(2,1)S(1)}, bf16[512,256]{1,0:T(8,128)(2,1)S(1)}, u32[]{:S(2)}, u32[]{:S(2)}) collective-permute-start(bf16[512,256]{1,0:T(8,128)(2,1)S(1)} %column.1.column_ref), channel_id=1, source_target_pairs={{0,1},{1,0},{2,3},{3,2},{4,5},{5,4},{6,7},{7,6},{8,9},{9,8},{10,11... | collective-permute-start | bytes 786440 | tf_op jit(solution)/shard_map/ppermute | solution.py:266
  30.7 2.4 %collective-permute-start.10 = (bf16[512,256]{1,0:T(8,128)(2,1)S(1)}, bf16[512,256]{1,0:T(8,128)(2,1)S(1)}, u32[]{:S(2)}, u32[]{:S(2)}) collective-permute-start(bf16[512,256]{1,0:T(8,128)(2,1)S(1)} %hand.1.beside_ref), channel_id=1, source_target_pairs={{0,1},{1,0},{2,3},{3,2},{4,5},{5,4},{6,7},{7,6},{8,9},{9,8},{10,11... | collective-permute-start | bytes 786440 | tf_op jit(solution)/shard_map/ppermute | solution.py:266
where the time goes:
time: 35.6 us; the launch traced here: 35.3 us
  starting transfers between devices  14.5 us (41%)
  Pallas kernels  12.3 us (35%)
  waiting for transfers between devices  4.56 us (13%)
  local copies, waits for them, and re-layouts  2.93 us (8%)
  other arithmetic  0.76 us (2%)
    ppermute x11, starting transfers between devices, send(): return lax.ppermute(value, 'row', pairs)  14.5 us
    pallas_call x10, Pallas kernels, call(): pl.pallas_call(kernel, out_shape=outs, in_specs=specs, out_specs=(VMEM,)...  12.3 us
    ppermute x11, waiting for transfers between devices, send(): return lax.ppermute(value, 'row', pairs)  4.56 us
    unnamed x18, local copies, waits for them, and re-layouts  2.93 us
    select_n x1, other arithmetic, body(): index = jnp.where(live, which * leaves + near_list % leaves, 3 * leaves)  0.76 us
  transfers between devices with their start and end apart: 11, of which 2 were waited for; matrix products, arithmetic and copies ran while one was open for 2% of the time, Pallas kernels for 28%

commit v1 on v0

--- a/solution.py
+++ b/solution.py
@@ -47,12 +47,22 @@
     parent_ref[...] = total.astype(jnp.bfloat16)
 
 
-def join_kernel(*refs):
-    *pieces, _, out_ref = refs
-    at = 0
-    for ref in pieces:
-        out_ref[pl.ds(at, ref.shape[0]), :] = ref[...]
-        at += ref.shape[0]
+def unused_layer(place):
+    layer = (place >> 2) & 3
+    corner = place & 3
+    below = ((layer + 3) & 3) ^ layer
+    above = ((layer + 1) & 3) ^ layer
+    return jnp.where(corner == 1, below, jnp.where(corner == 2, above, 0))
+
+
+def column_kernel(own_ref, first_ref, second_ref, third_ref, _, column_ref, sent_ref):
+    rank = own_ref.shape[0]
+    for n, ref in enumerate((own_ref, first_ref, second_ref, third_ref)):
+        column_ref[pl.ds(n * rank, rank), :] = ref[...]
+    unused = unused_layer(lax.axis_index("row") ^ 2)
+    for n in range(GROUP // 4 - 1):
+        index = jnp.where(n < unused, n, n + 1)
+        sent_ref[pl.ds(n * rank, rank), :] = column_ref[rows_at(index, rank), :]
 
 
 def pick_kernel(level_ref, layer_ref, out_ref):
@@ -202,12 +212,22 @@
 ):
     leaves, rows, rank = row_ref.shape
     local = lax.axis_index("row") & (GROUP - 1)
+    unused, their_unused = unused_layer(local), unused_layer(local ^ 1)
 
     def panel_of(slot):
         flip = (list_ref[0, slot] & (GROUP - 1)) ^ local
-        where = rows_at(flip >> 2, rank)
-        mine = jnp.where((flip & 2) == 0, column_ref[where, :], beside_ref[where, :])
-        theirs = jnp.where((flip & 2) == 0, their_column_ref[where, :], their_beside_ref[where, :])
+        layer = flip >> 2
+
+        def beside(ref, gap):
+            index = jnp.minimum(jnp.where(layer > gap, layer - 1, layer), GROUP // 4 - 2)
+            return ref[rows_at(index, rank), :]
+
+        where = rows_at(layer, rank)
+        same = (flip & 2) == 0
+        mine = jnp.where(same, column_ref[where, :], beside(beside_ref, unused))
+        theirs = jnp.where(
+            same, their_column_ref[where, :], beside(their_beside_ref, their_unused)
+        )
         return jnp.where((flip & 1) == 0, mine, theirs)
 
     terms = []
@@ -301,12 +321,14 @@
     near = call(
         near_kernel, "near", shape, [SMEM] + [ANY] * 3,
         (index, near_blocks, share, share_other),
-        scratch=slots_scratch(2 * leaves + 1), flops=10**9, limit=48,
+        scratch=slots_scratch(2 * leaves + 1), flops=2*10**9, limit=48,
     )
     layer = send(level, lambda d: d - 4 if d & 2 else d + 4)
-    column = call(join_kernel, "column", panel(GROUP // 4), [VMEM] * 4 + [ANY],
-        (parent, *layers, near))
-    beside = send(column, lambda d: d ^ 2)
+    column, sent = call(
+        column_kernel, "column", (panel(GROUP // 4), panel(GROUP // 4 - 1)),
+        [VMEM] * 4 + [ANY], (parent, *layers, near),
+    )
+    beside = send(sent, lambda d: d ^ 2)
     their_column = send(column, lambda d: d ^ 1)
     near = call(
         across_kernel, "across", shape, [SMEM, ANY, VMEM, ANY],
@@ -327,7 +349,7 @@
         flops=2 * leaves * far_slots * rank * rank * width,
         moved=2 * leaves * far_slots * rank * rank, limit=10,
     )
-    handed = call(hand_kernel, "hand", panel(GROUP // 4), [VMEM, ANY], (beside, near))
+    handed = call(hand_kernel, "hand", panel(GROUP // 4 - 1), [VMEM, ANY], (beside, near))
     their_beside = send(handed, lambda d: d ^ 1)
     return call(
         down_kernel, "down", jax.ShapeDtypeStruct(source.shape, jnp.bfloat16),

time: 35.6 us -> 34.8 us (0.978)
  the two profiles are of different devices: /device:TPU:27 before, /device:TPU:9 now
where the time goes in v1:
time: 34.8 us; the launch traced here: 34.3 us
  starting transfers between devices  13.4 us (39%)
  Pallas kernels  13.2 us (38%)
  waiting for transfers between devices  3.72 us (11%)
  local copies, waits for them, and re-layouts  2.93 us (8%)
  other arithmetic  0.76 us (2%)
    ppermute x11, starting transfers between devices, send(): return lax.ppermute(value, 'row', pairs)  13.4 us
    pallas_call x10, Pallas kernels, call(): pl.pallas_call(kernel, out_shape=outs, in_specs=specs, out_specs=(VMEM,)...  13.2 us
    ppermute x11, waiting for transfers between devices, send(): return lax.ppermute(value, 'row', pairs)  3.72 us
    unnamed x18, local copies, waits for them, and re-layouts  2.93 us
    select_n x1, other arithmetic, body(): index = jnp.where(live, which * leaves + near_list % leaves, 3 * leaves)  0.76 us
  transfers between devices with their start and end apart: 11, of which 2 were waited for; matrix products, arithmetic and copies ran while one was open for 2% of the time, Pallas kernels for 32%

profile of v1, /device:TPU:9, one launch (start us, length us, event | category | flops | bytes accessed | tf_op | source)
XLA Modules:
  0.0 34.3 jit_solution(10550149448422040276)
XLA Ops:
  0.0 0.0 copy-start.3
  0.0 1.0 %copy-done.3 = bf16[1024,256]{1,0:T(8,128)(2,1)S(1)} copy-done((bf16[1024,256]{1,0:T(8,128)(2,1)S(1)}, bf16[1024,256]{1,0:T(8,128)(2,1)}, u32[]{:S(2)}) %copy-start.3) | copy-done | bytes 524312
  1.0 0.0 copy-start.4
  1.0 0.9 %copy-done.4 = bf16[4,256,128]{2,1,0:T(8,128)(2,1)S(1)} copy-done((bf16[4,256,128]{2,1,0:T(8,128)(2,1)S(1)}, bf16[4,256,128]{2,1,0:T(8,128)(2,1)}, u32[]{:S(2)}) %copy-start.4) | copy-done | bytes 262168
  2.0 0.3 coef.1
  2.3 0.7 %collective-permute-start = (bf16[1536,256]{1,0:T(8,128)(2,1)S(1)}, bf16[1536,256]{1,0:T(8,128)(2,1)S(1)}, u32[]{:S(2)}, u32[]{:S(2)}) collective-permute-start(bf16[1536,256]{1,0:T(8,128)(2,1)S(1)} %get-tuple-element.9.own_ref.in_ref), channel_id=1, source_target_pairs={{0,1},{1,0},{2,3},{3,2},{4,5},{5,4},{6,7},{7,6},{8,9},{9,8},{10,11... | collective-permute-start | bytes 2359304 | tf_op jit(solution)/shard_map/ppermute | solution.py:286
  3.0 1.3 %collective-permute-start.2 = (bf16[512,256]{1,0:T(8,128)(2,1)S(1)}, bf16[512,256]{1,0:T(8,128)(2,1)S(1)}, u32[]{:S(2)}, u32[]{:S(2)}) collective-permute-start(bf16[512,256]{1,0:T(8,128)(2,1)S(1)} %get-tuple-element.10.coef_ref), channel_id=1, source_target_pairs={{0,2},{1,3},{2,0},{3,1},{4,6},{5,7},{6,4},{7,5},{8,10},{9,11},{10,... | collective-permute-start | bytes 786440 | tf_op jit(solution)/shard_map/ppermute | solution.py:286
  4.3 0.0 copy-start.1
  4.3 0.9 %copy-done.1 = bf16[4,128,128]{2,1,0:T(8,128)(2,1)S(1)} copy-done((bf16[4,128,128]{2,1,0:T(8,128)(2,1)S(1)}, bf16[4,128,128]{2,1,0:T(8,128)(2,1)}, u32[]{:S(2)}) %copy-start.1) | copy-done | bytes 131096
  5.2 0.3 parent.1.own_ref
  5.4 1.4 %collective-permute-start.7 = (bf16[128,256]{1,0:T(8,128)(2,1)S(1)}, bf16[128,256]{1,0:T(8,128)(2,1)S(1)}, u32[]{:S(2)}, u32[]{:S(2)}) collective-permute-start(bf16[128,256]{1,0:T(8,128)(2,1)S(1)} %parent.1.own_ref), channel_id=1, source_target_pairs={{0,12},{1,13},{2,14},{3,15},{4,8},{5,9},{6,10},{7,11},{8,4},{9,5},... | collective-permute-start | bytes 196616 | tf_op jit(solution)/shard_map/ppermute | solution.py:286
  6.8 1.1 %collective-permute-start.6 = (bf16[128,256]{1,0:T(8,128)(2,1)S(1)}, bf16[128,256]{1,0:T(8,128)(2,1)S(1)}, u32[]{:S(2)}, u32[]{:S(2)}) collective-permute-start(bf16[128,256]{1,0:T(8,128)(2,1)S(1)} %parent.1.own_ref), channel_id=1, source_target_pairs={{0,8},{1,9},{2,10},{3,11},{4,12},{5,13},{6,14},{7,15},{8,0},{9,1},... | collective-permute-start | bytes 196616 | tf_op jit(solution)/shard_map/ppermute | solution.py:286
  7.9 1.1 %collective-permute-start.5 = (bf16[128,256]{1,0:T(8,128)(2,1)S(1)}, bf16[128,256]{1,0:T(8,128)(2,1)S(1)}, u32[]{:S(2)}, u32[]{:S(2)}) collective-permute-start(bf16[128,256]{1,0:T(8,128)(2,1)S(1)} %parent.1.own_ref), channel_id=1, source_target_pairs={{0,4},{1,5},{2,6},{3,7},{4,0},{5,1},{6,2},{7,3},{8,12},{9,13},{10,... | collective-permute-start | bytes 196616 | tf_op jit(solution)/shard_map/ppermute | solution.py:286
  9.0 0.0 collective-permute-done.share_ref.refs_0_
  9.0 2.9 %collective-permute-start.1 = (bf16[1024,256]{1,0:T(8,128)(2,1)S(1)}, bf16[1024,256]{1,0:T(8,128)(2,1)S(1)}, u32[]{:S(2)}, u32[]{:S(2)}) collective-permute-start(bf16[1024,256]{1,0:T(8,128)(2,1)S(1)} %panels.1), channel_id=1, source_target_pairs={{1,2},{2,1},{3,4},{4,3},{5,6},{6,5},{7,8},{8,7},{9,10},{10,9},{11,... | collective-permute-start | bytes 1572872 | tf_op jit(solution)/shard_map/ppermute | solution.py:286
  12.0 0.8 %fusion.4.index_ref = s32[4,16]{1,0:T(4,128)S(1)} fusion(s32[4,16]{1,0:T(4,128)} %param.13, s32[]{:T(128)S(6)} %axis_index.12, s32[4]{0:T(128)} %param.14), kind=kLoop, calls=%fused_computation.9 | loop fusion | flops 1600 | bytes 532 | tf_op jit(solution)/shard_map/jit(_where)/select_n | solution.py:310
  12.7 0.0 collective-permute-done.2.level_ref
  12.7 3.1 %collective-permute-start.3 = (bf16[512,256]{1,0:T(8,128)(2,1)S(1)}, bf16[512,256]{1,0:T(8,128)(2,1)S(1)}, u32[]{:S(2)}, u32[]{:S(2)}) collective-permute-start(bf16[512,256]{1,0:T(8,128)(2,1)S(1)} %collective-permute-done.2.level_ref), channel_id=1, source_target_pairs={{0,4},{1,5},{4,8},{5,9},{6,2},{7,3},{8,12},{9,13},{10,6},{11,7},{1... | collective-permute-start | bytes 786440 | tf_op jit(solution)/shard_map/ppermute | solution.py:286
  15.8 5.2 %near.1.near_ref._ = f32[4,256,256]{2,1,0:T(8,128)S(1)} custom-call(s32[4,16]{1,0:T(4,128)S(1)} %fusion.4.index_ref, bf16[4,16,256,256]{3,2,1,0:T(8,128)(2,1)} %blocks_hbm.3, bf16[1536,256]{1,0:T(8,128)(2,1)S(1)} %get-tuple-element.9.own_ref.in_ref, bf16[1536,256]{1,0:T(8,128)(2,1)S(1)} %collective-permute-done.share_ref.refs_0_), custom_call_target="tpu_custom_call" | custom-call | flops 2000000000 | tf_op jit(solution)/shard_map/near/pallas_call | solution.py:253
  21.0 0.0 copy-start
  21.0 0.0 copy-start.7
  21.0 0.0 collective-permute-done.7.third_ref
  21.0 0.0 collective-permute-done.6.second_ref
  21.0 0.0 collective-permute-done.5.first_ref
  21.1 1.0 %collective-permute-start.8 = (bf16[384,256]{1,0:T(8,128)(2,1)S(1)}, bf16[384,256]{1,0:T(8,128)(2,1)S(1)}, u32[]{:S(2)}, u32[]{:S(2)}) collective-permute-start(bf16[384,256]{1,0:T(8,128)(2,1)S(1)} %get-tuple-element.12), channel_id=1, source_target_pairs={{0,2},{1,3},{2,0},{3,1},{4,6},{5,7},{6,4},{7,5},{8,10},{9,11},{10,... | collective-permute-start | bytes 589832 | tf_op jit(solution)/shard_map/ppermute | solution.py:286
  22.1 0.6 %collective-permute-done.3.layer_ref = bf16[512,256]{1,0:T(8,128)(2,1)S(1)} collective-permute-done((bf16[512,256]{1,0:T(8,128)(2,1)S(1)}, bf16[512,256]{1,0:T(8,128)(2,1)S(1)}, u32[]{:S(2)}, u32[]{:S(2)}) %collective-permute-start.3) | collective-permute-done | bytes 262176 | tf_op jit(solution)/shard_map/ppermute | solution.py:286
  22.7 0.0 copy-start.2
  22.7 0.0 copy-start.5
  22.7 0.0 copy-start.6
  22.7 0.0 copy-start.8
  22.7 0.7 %collective-permute-start.4 = (bf16[512,256]{1,0:T(8,128)(2,1)S(1)}, bf16[512,256]{1,0:T(8,128)(2,1)S(1)}, u32[]{:S(2)}, u32[]{:S(2)}) collective-permute-start(bf16[512,256]{1,0:T(8,128)(2,1)S(1)} %pick.1), channel_id=1, source_target_pairs={{0,1},{1,0},{2,3},{3,2},{4,5},{5,4},{6,7},{7,6},{8,9},{9,8},{10,11... | collective-permute-start | bytes 786440 | tf_op jit(solution)/shard_map/ppermute | solution.py:286
  23.5 0.1 collective-permute-start.9
  23.6 3.1 %collective-permute-done.1.across_ref = bf16[1024,256]{1,0:T(8,128)(2,1)S(1)} collective-permute-done((bf16[1024,256]{1,0:T(8,128)(2,1)S(1)}, bf16[1024,256]{1,0:T(8,128)(2,1)S(1)}, u32[]{:S(2)}, u32[]{:S(2)}) %collective-permute-start.1) | collective-permute-done | bytes 524320 | tf_op jit(solution)/shard_map/ppermute | solution.py:286
  26.7 3.8 %across.1.refs_0_.near_ref = f32[4,256,256]{2,1,0:T(8,128)S(1)} custom-call(s32[4,16]{1,0:T(4,128)S(1)} %fusion.4.index_ref, bf16[4,16,256,256]{3,2,1,0:T(8,128)(2,1)} %blocks_hbm.3, f32[4,256,256]{2,1,0:T(8,128)S(1)} %near.1.near_ref._, bf16[1024,256]{1,0:T(8,128)(2,1)S(1)} %collective-permute-done.1.across_ref), custom_call_target="tpu_custom_call" | custom-call | tf_op jit(solution)/shard_map/across/pallas_call | solution.py:253
  30.5 0.0 collective-permute-done.8.in_ref
  30.5 0.1 collective-permute-start.10
  30.6 0.0 collective-permute-done.4.passed_ref
  30.6 0.0 copy-done
  30.6 0.0 copy-done.7
  30.6 1.5 %far.1.far_ref = f32[512,256]{1,0:T(8,128)S(1)} custom-call(s32[4,16]{1,0:T(4,128)S(1)} %copy-done.7, bf16[4,16,128,128]{3,2,1,0:T(8,128)(2,1)S(1)} %copy-done, bf16[512,256]{1,0:T(8,128)(2,1)S(1)} %collective-permute-done.2.level_ref, bf16[512,256]{1,0:T(8,128)(2,1)S(1)} %collective-permute-done.3.layer_ref, ...), custom_call_target="tpu_custom_call" | custom-call | flops 536870912 | bytes 2097152 | tf_op jit(solution)/shard_map/far/pallas_call | solution.py:253
  32.1 0.0 collective-permute-done.9.their_column_ref
  32.1 0.0 collective-permute-done.10.their_beside_ref
  32.1 0.0 copy-done.2
  32.1 0.0 copy-done.5
  32.1 0.0 copy-done.6
  32.1 0.0 copy-done.8
  32.2 2.2 %down.1 = bf16[1024,256]{1,0:T(8,128)(2,1)} custom-call(s32[1,8]{1,0:T(1,128)S(1)} %copy-done.8, bf16[4,128,128]{2,1,0:T(8,128)(2,1)S(1)} %copy-done.2, bf16[1,8,128,128]{3,2,1,0:T(8,128)(2,1)S(1)} %copy-done.5, bf16[4,256,128]{2,1,0:T(8,128)(2,1)S(1)} %copy-done.6, f32[4,256,256]{2,1,0:T(8,128)S(1)} %across.1.refs_0_.near_ref, f32[512,256]{1,0:T(8,128)S(1)} %far.1.far_ref, ...), custom_call_target="tpu_custom_call" | custom-call | flops 134217728 | bytes 1048576 | tf_op jit(solution)/shard_map/down/pallas_call | solution.py:253
  (4 shorter events, 0.1 us)
Async XLA Ops:
  0.0 1.0 %copy-start.3 = (bf16[1024,256]{1,0:T(8,128)(2,1)S(1)}, bf16[1024,256]{1,0:T(8,128)(2,1)}, u32[]{:S(2)}) copy-start(bf16[1024,256]{1,0:T(8,128)(2,1)} %source_ref.1) | copy-start | bytes 1572868
  1.0 0.9 %copy-start.4 = (bf16[4,256,128]{2,1,0:T(8,128)(2,1)S(1)}, bf16[4,256,128]{2,1,0:T(8,128)(2,1)}, u32[]{:S(2)}) copy-start(bf16[4,256,128]{2,1,0:T(8,128)(2,1)} %col_ref.1) | copy-start | bytes 786436
  2.3 6.7 %collective-permute-start = (bf16[1536,256]{1,0:T(8,128)(2,1)S(1)}, bf16[1536,256]{1,0:T(8,128)(2,1)S(1)}, u32[]{:S(2)}, u32[]{:S(2)}) collective-permute-start(bf16[1536,256]{1,0:T(8,128)(2,1)S(1)} %get-tuple-element.9.own_ref.in_ref), channel_id=1, source_target_pairs={{0,1},{1,0},{2,3},{3,2},{4,5},{5,4},{6,7},{7,6},{8,9},{9,8},{10,11... | collective-permute-start | bytes 2359304 | tf_op jit(solution)/shard_map/ppermute | solution.py:286
  3.0 9.7 %collective-permute-start.2 = (bf16[512,256]{1,0:T(8,128)(2,1)S(1)}, bf16[512,256]{1,0:T(8,128)(2,1)S(1)}, u32[]{:S(2)}, u32[]{:S(2)}) collective-permute-start(bf16[512,256]{1,0:T(8,128)(2,1)S(1)} %get-tuple-element.10.coef_ref), channel_id=1, source_target_pairs={{0,2},{1,3},{2,0},{3,1},{4,6},{5,7},{6,4},{7,5},{8,10},{9,11},{10,... | collective-permute-start | bytes 786440 | tf_op jit(solution)/shard_map/ppermute | solution.py:286
  4.3 0.9 %copy-start.1 = (bf16[4,128,128]{2,1,0:T(8,128)(2,1)S(1)}, bf16[4,128,128]{2,1,0:T(8,128)(2,1)}, u32[]{:S(2)}) copy-start(bf16[4,128,128]{2,1,0:T(8,128)(2,1)} %transfer_ref.3) | copy-start | bytes 393220
  5.4 15.6 %collective-permute-start.7 = (bf16[128,256]{1,0:T(8,128)(2,1)S(1)}, bf16[128,256]{1,0:T(8,128)(2,1)S(1)}, u32[]{:S(2)}, u32[]{:S(2)}) collective-permute-start(bf16[128,256]{1,0:T(8,128)(2,1)S(1)} %parent.1.own_ref), channel_id=1, source_target_pairs={{0,12},{1,13},{2,14},{3,15},{4,8},{5,9},{6,10},{7,11},{8,4},{9,5},... | collective-permute-start | bytes 196616 | tf_op jit(solution)/shard_map/ppermute | solution.py:286
  6.8 14.2 %collective-permute-start.6 = (bf16[128,256]{1,0:T(8,128)(2,1)S(1)}, bf16[128,256]{1,0:T(8,128)(2,1)S(1)}, u32[]{:S(2)}, u32[]{:S(2)}) collective-permute-start(bf16[128,256]{1,0:T(8,128)(2,1)S(1)} %parent.1.own_ref), channel_id=1, source_target_pairs={{0,8},{1,9},{2,10},{3,11},{4,12},{5,13},{6,14},{7,15},{8,0},{9,1},... | collective-permute-start | bytes 196616 | tf_op jit(solution)/shard_map/ppermute | solution.py:286
  7.9 13.1 %collective-permute-start.5 = (bf16[128,256]{1,0:T(8,128)(2,1)S(1)}, bf16[128,256]{1,0:T(8,128)(2,1)S(1)}, u32[]{:S(2)}, u32[]{:S(2)}) collective-permute-start(bf16[128,256]{1,0:T(8,128)(2,1)S(1)} %parent.1.own_ref), channel_id=1, source_target_pairs={{0,4},{1,5},{2,6},{3,7},{4,0},{5,1},{6,2},{7,3},{8,12},{9,13},{10,... | collective-permute-start | bytes 196616 | tf_op jit(solution)/shard_map/ppermute | solution.py:286
  9.0 17.6 %collective-permute-start.1 = (bf16[1024,256]{1,0:T(8,128)(2,1)S(1)}, bf16[1024,256]{1,0:T(8,128)(2,1)S(1)}, u32[]{:S(2)}, u32[]{:S(2)}) collective-permute-start(bf16[1024,256]{1,0:T(8,128)(2,1)S(1)} %panels.1), channel_id=1, source_target_pairs={{1,2},{2,1},{3,4},{4,3},{5,6},{6,5},{7,8},{8,7},{9,10},{10,9},{11,... | collective-permute-start | bytes 1572872 | tf_op jit(solution)/shard_map/ppermute | solution.py:286
  12.7 9.9 %collective-permute-start.3 = (bf16[512,256]{1,0:T(8,128)(2,1)S(1)}, bf16[512,256]{1,0:T(8,128)(2,1)S(1)}, u32[]{:S(2)}, u32[]{:S(2)}) collective-permute-start(bf16[512,256]{1,0:T(8,128)(2,1)S(1)} %collective-permute-done.2.level_ref), channel_id=1, source_target_pairs={{0,4},{1,5},{4,8},{5,9},{6,2},{7,3},{8,12},{9,13},{10,6},{11,7},{1... | collective-permute-start | bytes 786440 | tf_op jit(solution)/shard_map/ppermute | solution.py:286
  21.0 9.6 %copy-start = (bf16[4,16,128,128]{3,2,1,0:T(8,128)(2,1)S(1)}, bf16[4,16,128,128]{3,2,1,0:T(8,128)(2,1)}, u32[]{:S(2)}) copy-start(bf16[4,16,128,128]{3,2,1,0:T(8,128)(2,1)} %coupling_ref.2) | copy-start | bytes 6291460
  21.0 9.6 %copy-start.7 = (s32[4,16]{1,0:T(4,128)S(1)}, s32[4,16]{1,0:T(4,128)}, u32[]{:S(2)}) copy-start(s32[4,16]{1,0:T(4,128)} %list_ref.2) | copy-start | bytes 772
  21.1 9.4 %collective-permute-start.8 = (bf16[384,256]{1,0:T(8,128)(2,1)S(1)}, bf16[384,256]{1,0:T(8,128)(2,1)S(1)}, u32[]{:S(2)}, u32[]{:S(2)}) collective-permute-start(bf16[384,256]{1,0:T(8,128)(2,1)S(1)} %get-tuple-element.12), channel_id=1, source_target_pairs={{0,2},{1,3},{2,0},{3,1},{4,6},{5,7},{6,4},{7,5},{8,10},{9,11},{10,... | collective-permute-start | bytes 589832 | tf_op jit(solution)/shard_map/ppermute | solution.py:286
  22.7 9.4 %copy-start.2 = (bf16[4,128,128]{2,1,0:T(8,128)(2,1)S(1)}, bf16[4,128,128]{2,1,0:T(8,128)(2,1)}, u32[]{:S(2)}) copy-start(bf16[4,128,128]{2,1,0:T(8,128)(2,1)} %transfer_ref.3) | copy-start | bytes 393220
  22.7 9.4 %copy-start.5 = (bf16[1,8,128,128]{3,2,1,0:T(8,128)(2,1)S(1)}, bf16[1,8,128,128]{3,2,1,0:T(8,128)(2,1)}, u32[]{:S(2)}) copy-start(bf16[1,8,128,128]{3,2,1,0:T(8,128)(2,1)} %coupling_ref.3) | copy-start | bytes 786436
  22.7 9.4 %copy-start.6 = (bf16[4,256,128]{2,1,0:T(8,128)(2,1)S(1)}, bf16[4,256,128]{2,1,0:T(8,128)(2,1)}, u32[]{:S(2)}) copy-start(bf16[4,256,128]{2,1,0:T(8,128)(2,1)} %row_ref.1) | copy-start | bytes 786436
  22.7 9.4 %copy-start.8 = (s32[1,8]{1,0:T(1,128)S(1)}, s32[1,8]{1,0:T(1,128)}, u32[]{:S(2)}) copy-start(s32[1,8]{1,0:T(1,128)} %list_ref.3) | copy-start | bytes 100
  22.7 7.8 %collective-permute-start.4 = (bf16[512,256]{1,0:T(8,128)(2,1)S(1)}, bf16[512,256]{1,0:T(8,128)(2,1)S(1)}, u32[]{:S(2)}, u32[]{:S(2)}) collective-permute-start(bf16[512,256]{1,0:T(8,128)(2,1)S(1)} %pick.1), channel_id=1, source_target_pairs={{0,1},{1,0},{2,3},{3,2},{4,5},{5,4},{6,7},{7,6},{8,9},{9,8},{10,11... | collective-permute-start | bytes 786440 | tf_op jit(solution)/shard_map/ppermute | solution.py:286
  23.5 8.6 %collective-permute-start.9 = (bf16[512,256]{1,0:T(8,128)(2,1)S(1)}, bf16[512,256]{1,0:T(8,128)(2,1)S(1)}, u32[]{:S(2)}, u32[]{:S(2)}) collective-permute-start(bf16[512,256]{1,0:T(8,128)(2,1)S(1)} %get-tuple-element.11.column_ref), channel_id=1, source_target_pairs={{0,1},{1,0},{2,3},{3,2},{4,5},{5,4},{6,7},{7,6},{8,9},{9,8},{10,11... | collective-permute-start | bytes 786440 | tf_op jit(solution)/shard_map/ppermute | solution.py:286
  30.5 1.6 %collective-permute-start.10 = (bf16[384,256]{1,0:T(8,128)(2,1)S(1)}, bf16[384,256]{1,0:T(8,128)(2,1)S(1)}, u32[]{:S(2)}, u32[]{:S(2)}) collective-permute-start(bf16[384,256]{1,0:T(8,128)(2,1)S(1)} %hand.1.beside_ref), channel_id=1, source_target_pairs={{0,1},{1,0},{2,3},{3,2},{4,5},{5,4},{6,7},{7,6},{8,9},{9,8},{10,11... | collective-permute-start | bytes 589832 | tf_op jit(solution)/shard_map/ppermute | solution.py:286

commit v2 on v1

--- a/solution.py
+++ b/solution.py
@@ -6,7 +6,7 @@
 from jax.sharding import PartitionSpec as P
 
 GROUP = 16
-CHUNK = 4
+CHUNK = 2
 MIB = 2**20
 
 VMEM = pl.BlockSpec(memory_space=pltpu.VMEM)
@@ -120,9 +120,7 @@
                         pltpu.make_async_copy(
                             blocks_hbm.at[leaf, 0], blocks.at[leaf, n], sems.at[leaf, n]
                         ).wait()
-                even = term(first) + term(first + 2)
-                odd = term(first + 1) + term(first + 3)
-                total_ref[leaf] = total_ref[leaf] + (even + odd)
+                total_ref[leaf] = total_ref[leaf] + (term(first) + term(first + 1))
 
 
 def near_kernel(
@@ -208,7 +206,8 @@
 def down_kernel(
     list_ref, transfer_ref, coupling_ref, row_ref, near_ref, far_ref,
     column_ref, beside_ref, their_column_ref, their_beside_ref,
-    out_ref,
+    out_hbm,
+    out, sems,
 ):
     leaves, rows, rank = row_ref.shape
     local = lax.axis_index("row") & (GROUP - 1)
@@ -243,18 +242,24 @@
         jnp.concatenate([matrix, matrix], axis=1), jnp.concatenate([high, low], axis=0)
     )
     down = (far_ref[...] + spread).astype(jnp.bfloat16)
+    copies = []
     for leaf in range(leaves):
         result = near_ref[leaf] + dot(row_ref[leaf], down[leaf * rank:(leaf + 1) * rank])
-        out_ref[pl.ds(leaf * rows, rows), :] = result.astype(jnp.bfloat16)
-
-
-def call(kernel, name, outs, specs, args, scratch=(), flops=0, moved=0, limit=4):
+        here = pl.ds(leaf * rows, rows)
+        out[here, :] = result.astype(jnp.bfloat16)
+        copies.append(pltpu.make_async_copy(out.at[here], out_hbm.at[here], sems.at[leaf]))
+        copies[-1].start()
+    for copy in copies:
+        copy.wait()
+
+
+def call(kernel, name, outs, specs, args, scratch=(), flops=0, moved=0, limit=4, to=VMEM):
     many = isinstance(outs, tuple)
     return pl.pallas_call(
         kernel,
         out_shape=outs,
         in_specs=specs,
-        out_specs=(VMEM,) * len(outs) if many else VMEM,
+        out_specs=(to,) * len(outs) if many else to,
         scratch_shapes=list(scratch),
         cost_estimate=pl.CostEstimate(flops=flops, bytes_accessed=moved, transcendentals=0),
         compiler_params=pltpu.CompilerParams(vmem_limit_bytes=limit * MIB),
@@ -359,7 +364,11 @@
             column, handed, their_column, their_beside,
         ),
         flops=8 * leaves * rank * rank * width,
-        moved=4 * leaves * rows * width, limit=8,
+        scratch=[
+            pltpu.VMEM(source.shape, jnp.bfloat16),
+            pltpu.SemaphoreType.DMA((leaves,)),
+        ],
+        moved=4 * leaves * rows * width, limit=8, to=ANY,
     )
 
 

time: 34.8 us -> 34.7 us (level)
  the two profiles are of different devices: /device:TPU:9 before, /device:TPU:1 now
where the time goes in v2:
time: 34.7 us; the launch traced here: 34.2 us
  starting transfers between devices  15.3 us (44%)
  Pallas kernels  13.9 us (40%)
  local copies, waits for them, and re-layouts  2.93 us (8%)
  waiting for transfers between devices  1.19 us (3%)
  other arithmetic  0.76 us (2%)
    ppermute x11, starting transfers between devices, send(): return lax.ppermute(value, 'row', pairs)  15.3 us
    pallas_call x10, Pallas kernels, call(): pl.pallas_call(kernel, out_shape=outs, in_specs=specs, out_specs=(to,) *...  13.9 us
    unnamed x18, local copies, waits for them, and re-layouts  2.93 us
    ppermute x11, waiting for transfers between devices, send(): return lax.ppermute(value, 'row', pairs)  1.19 us
    select_n x1, other arithmetic, body(): index = jnp.where(live, which * leaves + near_list % leaves, 3 * leaves)  0.76 us
  transfers between devices with their start and end apart: 11, of which 2 were waited for; matrix products, arithmetic and copies ran while one was open for 2% of the time, Pallas kernels for 34%

profile of v2, /device:TPU:1, one launch (start us, length us, event | category | flops | bytes accessed | tf_op | source)
XLA Modules:
  0.0 34.2 jit_solution(6504511612188362748)
XLA Ops:
  0.0 0.0 copy-start.3
  0.0 1.0 %copy-done.3 = bf16[1024,256]{1,0:T(8,128)(2,1)S(1)} copy-done((bf16[1024,256]{1,0:T(8,128)(2,1)S(1)}, bf16[1024,256]{1,0:T(8,128)(2,1)}, u32[]{:S(2)}) %copy-start.3) | copy-done | bytes 524312
  1.0 0.0 copy-start.4
  1.0 0.9 %copy-done.4 = bf16[4,256,128]{2,1,0:T(8,128)(2,1)S(1)} copy-done((bf16[4,256,128]{2,1,0:T(8,128)(2,1)S(1)}, bf16[4,256,128]{2,1,0:T(8,128)(2,1)}, u32[]{:S(2)}) %copy-start.4) | copy-done | bytes 262168
  2.0 0.3 coef.1
  2.3 0.1 collective-permute-start
  2.4 2.7 %collective-permute-start.2 = (bf16[512,256]{1,0:T(8,128)(2,1)S(1)}, bf16[512,256]{1,0:T(8,128)(2,1)S(1)}, u32[]{:S(2)}, u32[]{:S(2)}) collective-permute-start(bf16[512,256]{1,0:T(8,128)(2,1)S(1)} %get-tuple-element.10.coef_ref), channel_id=1, source_target_pairs={{0,2},{1,3},{2,0},{3,1},{4,6},{5,7},{6,4},{7,5},{8,10},{9,11},{10,... | collective-permute-start | bytes 786440 | tf_op jit(solution)/shard_map/ppermute | solution.py:291
  5.1 0.0 copy-start.1
  5.1 0.9 %copy-done.1 = bf16[4,128,128]{2,1,0:T(8,128)(2,1)S(1)} copy-done((bf16[4,128,128]{2,1,0:T(8,128)(2,1)S(1)}, bf16[4,128,128]{2,1,0:T(8,128)(2,1)}, u32[]{:S(2)}) %copy-start.1) | copy-done | bytes 131096
  6.0 0.2 parent.1.own_ref
  6.3 3.4 %collective-permute-start.7 = (bf16[128,256]{1,0:T(8,128)(2,1)S(1)}, bf16[128,256]{1,0:T(8,128)(2,1)S(1)}, u32[]{:S(2)}, u32[]{:S(2)}) collective-permute-start(bf16[128,256]{1,0:T(8,128)(2,1)S(1)} %parent.1.own_ref), channel_id=1, source_target_pairs={{0,12},{1,13},{2,14},{3,15},{4,8},{5,9},{6,10},{7,11},{8,4},{9,5},... | collective-permute-start | bytes 196616 | tf_op jit(solution)/shard_map/ppermute | solution.py:291
  9.6 0.0 collective-permute-start.6
  9.6 0.4 %collective-permute-start.5 = (bf16[128,256]{1,0:T(8,128)(2,1)S(1)}, bf16[128,256]{1,0:T(8,128)(2,1)S(1)}, u32[]{:S(2)}, u32[]{:S(2)}) collective-permute-start(bf16[128,256]{1,0:T(8,128)(2,1)S(1)} %parent.1.own_ref), channel_id=1, source_target_pairs={{0,4},{1,5},{2,6},{3,7},{4,0},{5,1},{6,2},{7,3},{8,12},{9,13},{10,... | collective-permute-start | bytes 196616 | tf_op jit(solution)/shard_map/ppermute | solution.py:291
  10.0 0.0 collective-permute-done.share_ref.refs_0_
  10.0 2.9 %collective-permute-start.1 = (bf16[1024,256]{1,0:T(8,128)(2,1)S(1)}, bf16[1024,256]{1,0:T(8,128)(2,1)S(1)}, u32[]{:S(2)}, u32[]{:S(2)}) collective-permute-start(bf16[1024,256]{1,0:T(8,128)(2,1)S(1)} %panels.1), channel_id=1, source_target_pairs={{1,2},{2,1},{3,4},{4,3},{5,6},{6,5},{7,8},{8,7},{9,10},{10,9},{11,... | collective-permute-start | bytes 1572872 | tf_op jit(solution)/shard_map/ppermute | solution.py:291
  13.0 0.8 %fusion.4.index_ref = s32[4,16]{1,0:T(4,128)S(1)} fusion(s32[4,16]{1,0:T(4,128)} %param.13, s32[]{:T(128)S(6)} %axis_index.12, s32[4]{0:T(128)} %param.14), kind=kLoop, calls=%fused_computation.9 | loop fusion | flops 1600 | bytes 532 | tf_op jit(solution)/shard_map/jit(_where)/select_n | solution.py:315
  13.7 0.0 collective-permute-done.2.level_ref
  13.7 3.0 %collective-permute-start.3 = (bf16[512,256]{1,0:T(8,128)(2,1)S(1)}, bf16[512,256]{1,0:T(8,128)(2,1)S(1)}, u32[]{:S(2)}, u32[]{:S(2)}) collective-permute-start(bf16[512,256]{1,0:T(8,128)(2,1)S(1)} %collective-permute-done.2.level_ref), channel_id=1, source_target_pairs={{0,4},{1,5},{4,8},{5,9},{6,2},{7,3},{8,12},{9,13},{10,6},{11,7},{1... | collective-permute-start | bytes 786440 | tf_op jit(solution)/shard_map/ppermute | solution.py:291
  16.8 6.3 %near.1.near_ref._ = f32[4,256,256]{2,1,0:T(8,128)S(1)} custom-call(s32[4,16]{1,0:T(4,128)S(1)} %fusion.4.index_ref, bf16[4,16,256,256]{3,2,1,0:T(8,128)(2,1)} %blocks_hbm.3, bf16[1536,256]{1,0:T(8,128)(2,1)S(1)} %get-tuple-element.9.own_ref.in_ref, bf16[1536,256]{1,0:T(8,128)(2,1)S(1)} %collective-permute-done.share_ref.refs_0_), custom_call_target="tpu_custom_call" | custom-call | flops 2000000000 | tf_op jit(solution)/shard_map/near/pallas_call | solution.py:258
  23.0 0.0 copy-start
  23.1 0.0 copy-start.7
  23.1 0.0 collective-permute-done.7.third_ref
  23.1 0.0 collective-permute-done.6.second_ref
  23.1 0.0 collective-permute-done.5.first_ref
  23.1 0.9 %collective-permute-start.8 = (bf16[384,256]{1,0:T(8,128)(2,1)S(1)}, bf16[384,256]{1,0:T(8,128)(2,1)S(1)}, u32[]{:S(2)}, u32[]{:S(2)}) collective-permute-start(bf16[384,256]{1,0:T(8,128)(2,1)S(1)} %get-tuple-element.12), channel_id=1, source_target_pairs={{0,2},{1,3},{2,0},{3,1},{4,6},{5,7},{6,4},{7,5},{8,10},{9,11},{10,... | collective-permute-start | bytes 589832 | tf_op jit(solution)/shard_map/ppermute | solution.py:291
  24.0 0.0 collective-permute-done.3.layer_ref
  24.0 0.0 copy-start.2
  24.1 0.0 copy-start.5
  24.1 0.0 copy-start.6
  24.1 0.0 copy-start.8
  24.1 0.1 collective-permute-start.4
  24.2 0.5 %collective-permute-start.9 = (bf16[512,256]{1,0:T(8,128)(2,1)S(1)}, bf16[512,256]{1,0:T(8,128)(2,1)S(1)}, u32[]{:S(2)}, u32[]{:S(2)}) collective-permute-start(bf16[512,256]{1,0:T(8,128)(2,1)S(1)} %get-tuple-element.11.column_ref), channel_id=1, source_target_pairs={{0,1},{1,0},{2,3},{3,2},{4,5},{5,4},{6,7},{7,6},{8,9},{9,8},{10,11... | collective-permute-start | bytes 786440 | tf_op jit(solution)/shard_map/ppermute | solution.py:291
  24.7 0.4 %collective-permute-done.1.across_ref = bf16[1024,256]{1,0:T(8,128)(2,1)S(1)} collective-permute-done((bf16[1024,256]{1,0:T(8,128)(2,1)S(1)}, bf16[1024,256]{1,0:T(8,128)(2,1)S(1)}, u32[]{:S(2)}, u32[]{:S(2)}) %collective-permute-start.1) | collective-permute-done | bytes 524320 | tf_op jit(solution)/shard_map/ppermute | solution.py:291
  25.0 3.4 %across.1.refs_0_.near_ref = f32[4,256,256]{2,1,0:T(8,128)S(1)} custom-call(s32[4,16]{1,0:T(4,128)S(1)} %fusion.4.index_ref, bf16[4,16,256,256]{3,2,1,0:T(8,128)(2,1)} %blocks_hbm.3, f32[4,256,256]{2,1,0:T(8,128)S(1)} %near.1.near_ref._, bf16[1024,256]{1,0:T(8,128)(2,1)S(1)} %collective-permute-done.1.across_ref), custom_call_target="tpu_custom_call" | custom-call | tf_op jit(solution)/shard_map/across/pallas_call | solution.py:258
  28.5 0.8 %collective-permute-done.8.in_ref = bf16[384,256]{1,0:T(8,128)(2,1)S(1)} collective-permute-done((bf16[384,256]{1,0:T(8,128)(2,1)S(1)}, bf16[384,256]{1,0:T(8,128)(2,1)S(1)}, u32[]{:S(2)}, u32[]{:S(2)}) %collective-permute-start.8) | collective-permute-done | bytes 196640 | tf_op jit(solution)/shard_map/ppermute | solution.py:291
  29.3 1.3 %collective-permute-start.10 = (bf16[384,256]{1,0:T(8,128)(2,1)S(1)}, bf16[384,256]{1,0:T(8,128)(2,1)S(1)}, u32[]{:S(2)}, u32[]{:S(2)}) collective-permute-start(bf16[384,256]{1,0:T(8,128)(2,1)S(1)} %hand.1.beside_ref), channel_id=1, source_target_pairs={{0,1},{1,0},{2,3},{3,2},{4,5},{5,4},{6,7},{7,6},{8,9},{9,8},{10,11... | collective-permute-start | bytes 589832 | tf_op jit(solution)/shard_map/ppermute | solution.py:291
  30.6 0.0 collective-permute-done.4.passed_ref
  30.6 0.0 copy-done
  30.6 0.0 copy-done.7
  30.6 1.5 %far.1.far_ref = f32[512,256]{1,0:T(8,128)S(1)} custom-call(s32[4,16]{1,0:T(4,128)S(1)} %copy-done.7, bf16[4,16,128,128]{3,2,1,0:T(8,128)(2,1)S(1)} %copy-done, bf16[512,256]{1,0:T(8,128)(2,1)S(1)} %collective-permute-done.2.level_ref, bf16[512,256]{1,0:T(8,128)(2,1)S(1)} %collective-permute-done.3.layer_ref, ...), custom_call_target="tpu_custom_call" | custom-call | flops 536870912 | bytes 2097152 | tf_op jit(solution)/shard_map/far/pallas_call | solution.py:258
  32.1 0.0 collective-permute-done.9.their_column_ref
  32.1 0.0 collective-permute-done.10.their_beside_ref
  32.1 0.0 copy-done.2
  32.1 0.0 copy-done.5
  32.1 0.0 copy-done.6
  32.2 0.0 copy-done.8
  32.2 2.1 %down.1 = bf16[1024,256]{1,0:T(8,128)(2,1)} custom-call(s32[1,8]{1,0:T(1,128)S(1)} %copy-done.8, bf16[4,128,128]{2,1,0:T(8,128)(2,1)S(1)} %copy-done.2, bf16[1,8,128,128]{3,2,1,0:T(8,128)(2,1)S(1)} %copy-done.5, bf16[4,256,128]{2,1,0:T(8,128)(2,1)S(1)} %copy-done.6, f32[4,256,256]{2,1,0:T(8,128)S(1)} %across.1.refs_0_.near_ref, f32[512,256]{1,0:T(8,128)S(1)} %far.1.far_ref, ...), custom_call_target="tpu_custom_call" | custom-call | flops 134217728 | bytes 1048576 | tf_op jit(solution)/shard_map/down/pallas_call | solution.py:258
  (4 shorter events, 0.1 us)
Async XLA Ops:
  0.0 1.0 %copy-start.3 = (bf16[1024,256]{1,0:T(8,128)(2,1)S(1)}, bf16[1024,256]{1,0:T(8,128)(2,1)}, u32[]{:S(2)}) copy-start(bf16[1024,256]{1,0:T(8,128)(2,1)} %source_ref.1) | copy-start | bytes 1572868
  1.0 0.9 %copy-start.4 = (bf16[4,256,128]{2,1,0:T(8,128)(2,1)S(1)}, bf16[4,256,128]{2,1,0:T(8,128)(2,1)}, u32[]{:S(2)}) copy-start(bf16[4,256,128]{2,1,0:T(8,128)(2,1)} %col_ref.1) | copy-start | bytes 786436
  2.3 7.7 %collective-permute-start = (bf16[1536,256]{1,0:T(8,128)(2,1)S(1)}, bf16[1536,256]{1,0:T(8,128)(2,1)S(1)}, u32[]{:S(2)}, u32[]{:S(2)}) collective-permute-start(bf16[1536,256]{1,0:T(8,128)(2,1)S(1)} %get-tuple-element.9.own_ref.in_ref), channel_id=1, source_target_pairs={{0,1},{1,0},{2,3},{3,2},{4,5},{5,4},{6,7},{7,6},{8,9},{9,8},{10,11... | collective-permute-start | bytes 2359304 | tf_op jit(solution)/shard_map/ppermute | solution.py:291
  2.4 11.3 %collective-permute-start.2 = (bf16[512,256]{1,0:T(8,128)(2,1)S(1)}, bf16[512,256]{1,0:T(8,128)(2,1)S(1)}, u32[]{:S(2)}, u32[]{:S(2)}) collective-permute-start(bf16[512,256]{1,0:T(8,128)(2,1)S(1)} %get-tuple-element.10.coef_ref), channel_id=1, source_target_pairs={{0,2},{1,3},{2,0},{3,1},{4,6},{5,7},{6,4},{7,5},{8,10},{9,11},{10,... | collective-permute-start | bytes 786440 | tf_op jit(solution)/shard_map/ppermute | solution.py:291
  5.1 0.9 %copy-start.1 = (bf16[4,128,128]{2,1,0:T(8,128)(2,1)S(1)}, bf16[4,128,128]{2,1,0:T(8,128)(2,1)}, u32[]{:S(2)}) copy-start(bf16[4,128,128]{2,1,0:T(8,128)(2,1)} %transfer_ref.3) | copy-start | bytes 393220
  6.3 16.8 %collective-permute-start.7 = (bf16[128,256]{1,0:T(8,128)(2,1)S(1)}, bf16[128,256]{1,0:T(8,128)(2,1)S(1)}, u32[]{:S(2)}, u32[]{:S(2)}) collective-permute-start(bf16[128,256]{1,0:T(8,128)(2,1)S(1)} %parent.1.own_ref), channel_id=1, source_target_pairs={{0,12},{1,13},{2,14},{3,15},{4,8},{5,9},{6,10},{7,11},{8,4},{9,5},... | collective-permute-start | bytes 196616 | tf_op jit(solution)/shard_map/ppermute | solution.py:291
  9.6 13.4 %collective-permute-start.6 = (bf16[128,256]{1,0:T(8,128)(2,1)S(1)}, bf16[128,256]{1,0:T(8,128)(2,1)S(1)}, u32[]{:S(2)}, u32[]{:S(2)}) collective-permute-start(bf16[128,256]{1,0:T(8,128)(2,1)S(1)} %parent.1.own_ref), channel_id=1, source_target_pairs={{0,8},{1,9},{2,10},{3,11},{4,12},{5,13},{6,14},{7,15},{8,0},{9,1},... | collective-permute-start | bytes 196616 | tf_op jit(solution)/shard_map/ppermute | solution.py:291
  9.6 13.4 %collective-permute-start.5 = (bf16[128,256]{1,0:T(8,128)(2,1)S(1)}, bf16[128,256]{1,0:T(8,128)(2,1)S(1)}, u32[]{:S(2)}, u32[]{:S(2)}) collective-permute-start(bf16[128,256]{1,0:T(8,128)(2,1)S(1)} %parent.1.own_ref), channel_id=1, source_target_pairs={{0,4},{1,5},{2,6},{3,7},{4,0},{5,1},{6,2},{7,3},{8,12},{9,13},{10,... | collective-permute-start | bytes 196616 | tf_op jit(solution)/shard_map/ppermute | solution.py:291
  10.0 15.0 %collective-permute-start.1 = (bf16[1024,256]{1,0:T(8,128)(2,1)S(1)}, bf16[1024,256]{1,0:T(8,128)(2,1)S(1)}, u32[]{:S(2)}, u32[]{:S(2)}) collective-permute-start(bf16[1024,256]{1,0:T(8,128)(2,1)S(1)} %panels.1), channel_id=1, source_target_pairs={{1,2},{2,1},{3,4},{4,3},{5,6},{6,5},{7,8},{8,7},{9,10},{10,9},{11,... | collective-permute-start | bytes 1572872 | tf_op jit(solution)/shard_map/ppermute | solution.py:291
  13.7 10.3 %collective-permute-start.3 = (bf16[512,256]{1,0:T(8,128)(2,1)S(1)}, bf16[512,256]{1,0:T(8,128)(2,1)S(1)}, u32[]{:S(2)}, u32[]{:S(2)}) collective-permute-start(bf16[512,256]{1,0:T(8,128)(2,1)S(1)} %collective-permute-done.2.level_ref), channel_id=1, source_target_pairs={{0,4},{1,5},{4,8},{5,9},{6,2},{7,3},{8,12},{9,13},{10,6},{11,7},{1... | collective-permute-start | bytes 786440 | tf_op jit(solution)/shard_map/ppermute | solution.py:291
  23.0 7.6 %copy-start = (bf16[4,16,128,128]{3,2,1,0:T(8,128)(2,1)S(1)}, bf16[4,16,128,128]{3,2,1,0:T(8,128)(2,1)}, u32[]{:S(2)}) copy-start(bf16[4,16,128,128]{3,2,1,0:T(8,128)(2,1)} %coupling_ref.2) | copy-start | bytes 6291460
  23.1 7.6 %copy-start.7 = (s32[4,16]{1,0:T(4,128)S(1)}, s32[4,16]{1,0:T(4,128)}, u32[]{:S(2)}) copy-start(s32[4,16]{1,0:T(4,128)} %list_ref.2) | copy-start | bytes 772
  23.1 6.1 %collective-permute-start.8 = (bf16[384,256]{1,0:T(8,128)(2,1)S(1)}, bf16[384,256]{1,0:T(8,128)(2,1)S(1)}, u32[]{:S(2)}, u32[]{:S(2)}) collective-permute-start(bf16[384,256]{1,0:T(8,128)(2,1)S(1)} %get-tuple-element.12), channel_id=1, source_target_pairs={{0,2},{1,3},{2,0},{3,1},{4,6},{5,7},{6,4},{7,5},{8,10},{9,11},{10,... | collective-permute-start | bytes 589832 | tf_op jit(solution)/shard_map/ppermute | solution.py:291
  24.0 8.1 %copy-start.2 = (bf16[4,128,128]{2,1,0:T(8,128)(2,1)S(1)}, bf16[4,128,128]{2,1,0:T(8,128)(2,1)}, u32[]{:S(2)}) copy-start(bf16[4,128,128]{2,1,0:T(8,128)(2,1)} %transfer_ref.3) | copy-start | bytes 393220
  24.1 8.1 %copy-start.5 = (bf16[1,8,128,128]{3,2,1,0:T(8,128)(2,1)S(1)}, bf16[1,8,128,128]{3,2,1,0:T(8,128)(2,1)}, u32[]{:S(2)}) copy-start(bf16[1,8,128,128]{3,2,1,0:T(8,128)(2,1)} %coupling_ref.3) | copy-start | bytes 786436
  24.1 8.1 %copy-start.6 = (bf16[4,256,128]{2,1,0:T(8,128)(2,1)S(1)}, bf16[4,256,128]{2,1,0:T(8,128)(2,1)}, u32[]{:S(2)}) copy-start(bf16[4,256,128]{2,1,0:T(8,128)(2,1)} %row_ref.1) | copy-start | bytes 786436
  24.1 8.1 %copy-start.8 = (s32[1,8]{1,0:T(1,128)S(1)}, s32[1,8]{1,0:T(1,128)}, u32[]{:S(2)}) copy-start(s32[1,8]{1,0:T(1,128)} %list_ref.3) | copy-start | bytes 100
  24.1 6.5 %collective-permute-start.4 = (bf16[512,256]{1,0:T(8,128)(2,1)S(1)}, bf16[512,256]{1,0:T(8,128)(2,1)S(1)}, u32[]{:S(2)}, u32[]{:S(2)}) collective-permute-start(bf16[512,256]{1,0:T(8,128)(2,1)S(1)} %pick.1), channel_id=1, source_target_pairs={{0,1},{1,0},{2,3},{3,2},{4,5},{5,4},{6,7},{7,6},{8,9},{9,8},{10,11... | collective-permute-start | bytes 786440 | tf_op jit(solution)/shard_map/ppermute | solution.py:291
  24.2 7.9 %collective-permute-start.9 = (bf16[512,256]{1,0:T(8,128)(2,1)S(1)}, bf16[512,256]{1,0:T(8,128)(2,1)S(1)}, u32[]{:S(2)}, u32[]{:S(2)}) collective-permute-start(bf16[512,256]{1,0:T(8,128)(2,1)S(1)} %get-tuple-element.11.column_ref), channel_id=1, source_target_pairs={{0,1},{1,0},{2,3},{3,2},{4,5},{5,4},{6,7},{7,6},{8,9},{9,8},{10,11... | collective-permute-start | bytes 786440 | tf_op jit(solution)/shard_map/ppermute | solution.py:291
  29.3 2.8 %collective-permute-start.10 = (bf16[384,256]{1,0:T(8,128)(2,1)S(1)}, bf16[384,256]{1,0:T(8,128)(2,1)S(1)}, u32[]{:S(2)}, u32[]{:S(2)}) collective-permute-start(bf16[384,256]{1,0:T(8,128)(2,1)S(1)} %hand.1.beside_ref), channel_id=1, source_target_pairs={{0,1},{1,0},{2,3},{3,2},{4,5},{5,4},{6,7},{7,6},{8,9},{9,8},{10,11... | collective-permute-start | bytes 589832 | tf_op jit(solution)/shard_map/ppermute | solution.py:291

commit v3 on v2

--- a/solution.py
+++ b/solution.py
@@ -28,14 +28,11 @@
     return pl.ds(pl.multiple_of(index * rows, rows), rows)
 
 
-def coef_kernel(source_ref, col_ref, share_ref, coef_ref):
+def coef_kernel(source_ref, col_ref, coef_ref):
     leaves, rows, rank = col_ref.shape
     for leaf in range(leaves):
         panel = source_ref[pl.ds(leaf * rows, rows), :]
-        share_ref[pl.ds(leaf * rows, rows), :] = panel
-        coef = dot_t(col_ref[leaf], panel).astype(jnp.bfloat16)
-        coef_ref[pl.ds(leaf * rank, rank), :] = coef
-        share_ref[pl.ds(leaves * rows + leaf * rank, rank), :] = coef
+        coef_ref[pl.ds(leaf * rank, rank), :] = dot_t(col_ref[leaf], panel).astype(jnp.bfloat16)
 
 
 def parent_kernel(coef_ref, transfer_ref, parent_ref):
@@ -55,10 +52,11 @@
     return jnp.where(corner == 1, below, jnp.where(corner == 2, above, 0))
 
 
-def column_kernel(own_ref, first_ref, second_ref, third_ref, _, column_ref, sent_ref):
+def column_kernel(own_ref, first_ref, second_ref, third_ref, coef_ref, _, column_ref, sent_ref):
     rank = own_ref.shape[0]
     for n, ref in enumerate((own_ref, first_ref, second_ref, third_ref)):
         column_ref[pl.ds(n * rank, rank), :] = ref[...]
+    column_ref[pl.ds(4 * rank, coef_ref.shape[0]), :] = coef_ref[...]
     unused = unused_layer(lax.axis_index("row") ^ 2)
     for n in range(GROUP // 4 - 1):
         index = jnp.where(n < unused, n, n + 1)
@@ -293,19 +291,18 @@
     def panel(blocks, dtype=jnp.bfloat16):
         return jax.ShapeDtypeStruct((blocks * rank, width), dtype)
 
-    share, coef = call(
-        coef_kernel, "coef",
-        (jax.ShapeDtypeStruct((leaves * (rows + rank), width), jnp.bfloat16), panel(leaves)),
-        [VMEM] * 2, (source, col_basis), flops=2 * leaves * rank * width * rows,
+    coef = call(
+        coef_kernel, "coef", panel(leaves), [VMEM] * 2, (source, col_basis),
+        flops=2 * leaves * rank * width * rows,
         moved=2 * leaves * rows * (width + rank), limit=8,
     )
     parent = call(parent_kernel, "parent", panel(1), [VMEM] * 2, (coef, transfer))
     layers = [send(parent, lambda d, bit=bit: d ^ bit) for bit in (4, 8, 12)]
-    share_other = send(share, lambda d: d ^ 1)
+    source_other = send(source, lambda d: d ^ 1)
     level = send(coef, lambda d: d ^ 2)
     panels = call(
         hand_kernel, "panels", jax.ShapeDtypeStruct(source.shape, jnp.bfloat16), [VMEM] + [ANY] * 1,
-        (share, share_other),
+        (source, source_other),
     )
     across = send(panels, lambda d: d + 1 if d & 1 else d - 1)
 
@@ -325,13 +322,13 @@
     shape = jax.ShapeDtypeStruct((leaves, rows, width), jnp.float32)
     near = call(
         near_kernel, "near", shape, [SMEM] + [ANY] * 3,
-        (index, near_blocks, share, share_other),
-        scratch=slots_scratch(2 * leaves + 1), flops=2*10**9, limit=48,
+        (index, near_blocks, panels, source_other),
+        scratch=slots_scratch(2 * leaves + 1), flops=10**9, limit=48,
     )
     layer = send(level, lambda d: d - 4 if d & 2 else d + 4)
     column, sent = call(
-        column_kernel, "column", (panel(GROUP // 4), panel(GROUP // 4 - 1)),
-        [VMEM] * 4 + [ANY], (parent, *layers, near),
+        column_kernel, "column", (panel(GROUP // 4 + leaves), panel(GROUP // 4 - 1)),
+        [VMEM] * 5 + [ANY], (parent, *layers, coef, near),
     )
     beside = send(sent, lambda d: d ^ 2)
     their_column = send(column, lambda d: d ^ 1)
@@ -346,7 +343,7 @@
     passed = send(picked_coef, lambda d: d ^ 1)
     far = call(
         far_kernel, "far", panel(leaves, jnp.float32), [SMEM, VMEM] + [ANY] * 4,
-        (far_list, far_coupling, level, layer, share_other, passed),
+        (far_list, far_coupling, level, layer, their_column, passed),
         scratch=[
             pltpu.VMEM((4 * leaves * rank, width), jnp.bfloat16),
             pltpu.SemaphoreType.DMA((4,)),

time: 34.7 us -> 36.7 us (1.058); the launches traced: 34.2 us -> 37.3 us
  starting transfers between devices: 15.3 us -> 16.5 us
  local copies, waits for them, and re-layouts: 2.93 us -> 3.97 us
  waiting for transfers between devices: 1.19 us -> 2.13 us
    ppermute x11, starting transfers between devices: 15.3 us -> 16.5 us  [send(): return lax.ppermute(value, 'row', pairs)]
    unnamed x18 -> x20, local copies, waits for them, and re-layouts: 2.93 us -> 3.97 us
    ppermute x11, waiting for transfers between devices: 1.19 us -> 2.13 us  [send(): return lax.ppermute(value, 'row', pairs)]
  transfers between devices with their start and end apart: 11 -> 11, of which waited for: 2 -> 1; matrix products, arithmetic and copies ran while one was open for 2% -> 2% of each run, Pallas kernels for 34% -> 31%
where the time goes in v3:
time: 36.7 us; the launch traced here: 37.3 us
  starting transfers between devices  16.5 us (45%)
  Pallas kernels  13.7 us (37%)
  local copies, waits for them, and re-layouts  3.97 us (11%)
  waiting for transfers between devices  2.13 us (6%)
  other arithmetic  0.76 us (2%)
    ppermute x11, starting transfers between devices, send(): return lax.ppermute(value, 'row', pairs)  16.5 us
    pallas_call x10, Pallas kernels, call(): pl.pallas_call(kernel, out_shape=outs, in_specs=specs, out_specs=(to,) *...  13.7 us
    unnamed x20, local copies, waits for them, and re-layouts  3.97 us
    ppermute x11, waiting for transfers between devices, send(): return lax.ppermute(value, 'row', pairs)  2.13 us
    select_n x1, other arithmetic, body(): index = jnp.where(live, which * leaves + near_list % leaves, 3 * leaves)  0.76 us
  transfers between devices with their start and end apart: 11, of which 1 were waited for; matrix products, arithmetic and copies ran while one was open for 2% of the time, Pallas kernels for 31%

profile of v3, /device:TPU:1, one launch (start us, length us, event | category | flops | bytes accessed | tf_op | source)
XLA Modules:
  0.0 37.3 jit_solution(2686796364549594149)
XLA Ops:
  0.0 0.1 collective-permute-start
  0.1 0.0 copy-start.1
  0.1 1.0 %copy-done.1 = bf16[1024,256]{1,0:T(8,128)(2,1)S(1)} copy-done((bf16[1024,256]{1,0:T(8,128)(2,1)S(1)}, bf16[1024,256]{1,0:T(8,128)(2,1)}, u32[]{:S(2)}) %copy-start.1) | copy-done | bytes 524312
  1.1 0.0 copy-start.7
  1.1 0.9 %copy-done.7 = bf16[4,256,128]{2,1,0:T(8,128)(2,1)S(1)} copy-done((bf16[4,256,128]{2,1,0:T(8,128)(2,1)S(1)}, bf16[4,256,128]{2,1,0:T(8,128)(2,1)}, u32[]{:S(2)}) %copy-start.7) | copy-done | bytes 262168
  2.1 0.3 coef.1.coef_ref
  2.3 2.8 %collective-permute-start.2 = (bf16[512,256]{1,0:T(8,128)(2,1)S(1)}, bf16[512,256]{1,0:T(8,128)(2,1)S(1)}, u32[]{:S(2)}, u32[]{:S(2)}) collective-permute-start(bf16[512,256]{1,0:T(8,128)(2,1)S(1)} %coef.1.coef_ref), channel_id=1, source_target_pairs={{0,2},{1,3},{2,0},{3,1},{4,6},{5,7},{6,4},{7,5},{8,10},{9,11},{10,... | collective-permute-start | bytes 786440 | tf_op jit(solution)/shard_map/ppermute | solution.py:289
  5.1 0.0 copy-start.3
  5.1 0.9 %copy-done.3 = bf16[4,128,128]{2,1,0:T(8,128)(2,1)S(1)} copy-done((bf16[4,128,128]{2,1,0:T(8,128)(2,1)S(1)}, bf16[4,128,128]{2,1,0:T(8,128)(2,1)}, u32[]{:S(2)}) %copy-start.3) | copy-done | bytes 131096
  6.0 0.2 parent.1.own_ref
  6.2 1.4 %collective-permute-start.4 = (bf16[128,256]{1,0:T(8,128)(2,1)S(1)}, bf16[128,256]{1,0:T(8,128)(2,1)S(1)}, u32[]{:S(2)}, u32[]{:S(2)}) collective-permute-start(bf16[128,256]{1,0:T(8,128)(2,1)S(1)} %parent.1.own_ref), channel_id=1, source_target_pairs={{0,4},{1,5},{2,6},{3,7},{4,0},{5,1},{6,2},{7,3},{8,12},{9,13},{10,... | collective-permute-start | bytes 196616 | tf_op jit(solution)/shard_map/ppermute | solution.py:289
  7.6 2.3 %collective-permute-start.5 = (bf16[128,256]{1,0:T(8,128)(2,1)S(1)}, bf16[128,256]{1,0:T(8,128)(2,1)S(1)}, u32[]{:S(2)}, u32[]{:S(2)}) collective-permute-start(bf16[128,256]{1,0:T(8,128)(2,1)S(1)} %parent.1.own_ref), channel_id=1, source_target_pairs={{0,8},{1,9},{2,10},{3,11},{4,12},{5,13},{6,14},{7,15},{8,0},{9,1},... | collective-permute-start | bytes 196616 | tf_op jit(solution)/shard_map/ppermute | solution.py:289
  9.9 0.0 collective-permute-start.6
  9.9 0.0 collective-permute-done.refs_0_.share_ref
  9.9 0.0 copy-start.2
  9.9 1.0 %copy-done.2 = bf16[1024,256]{1,0:T(8,128)(2,1)S(1)} copy-done((bf16[1024,256]{1,0:T(8,128)(2,1)S(1)}, bf16[1024,256]{1,0:T(8,128)(2,1)}, u32[]{:S(2)}) %copy-start.2) | copy-done | bytes 524312
  11.0 2.9 %collective-permute-start.1 = (bf16[1024,256]{1,0:T(8,128)(2,1)S(1)}, bf16[1024,256]{1,0:T(8,128)(2,1)S(1)}, u32[]{:S(2)}, u32[]{:S(2)}) collective-permute-start(bf16[1024,256]{1,0:T(8,128)(2,1)S(1)} %panels.1.own_ref), channel_id=1, source_target_pairs={{1,2},{2,1},{3,4},{4,3},{5,6},{6,5},{7,8},{8,7},{9,10},{10,9},{11,... | collective-permute-start | bytes 1572872 | tf_op jit(solution)/shard_map/ppermute | solution.py:289
  13.9 0.8 %fusion.4.index_ref = s32[4,16]{1,0:T(4,128)S(1)} fusion(s32[4,16]{1,0:T(4,128)} %param.13, s32[]{:T(128)S(6)} %axis_index.12, s32[4]{0:T(128)} %param.14), kind=kLoop, calls=%fused_computation.9 | loop fusion | flops 1600 | bytes 532 | tf_op jit(solution)/shard_map/jit(_where)/select_n | solution.py:312
  14.6 0.0 collective-permute-done.2.level_ref
  14.6 2.5 %collective-permute-start.3 = (bf16[512,256]{1,0:T(8,128)(2,1)S(1)}, bf16[512,256]{1,0:T(8,128)(2,1)S(1)}, u32[]{:S(2)}, u32[]{:S(2)}) collective-permute-start(bf16[512,256]{1,0:T(8,128)(2,1)S(1)} %collective-permute-done.2.level_ref), channel_id=1, source_target_pairs={{0,4},{1,5},{4,8},{5,9},{6,2},{7,3},{8,12},{9,13},{10,6},{11,7},{1... | collective-permute-start | bytes 786440 | tf_op jit(solution)/shard_map/ppermute | solution.py:289
  17.2 5.4 %near.1.near_ref._ = f32[4,256,256]{2,1,0:T(8,128)S(1)} custom-call(s32[4,16]{1,0:T(4,128)S(1)} %fusion.4.index_ref, bf16[4,16,256,256]{3,2,1,0:T(8,128)(2,1)} %blocks_hbm.3, bf16[1024,256]{1,0:T(8,128)(2,1)S(1)} %panels.1.own_ref, bf16[1024,256]{1,0:T(8,128)(2,1)S(1)} %collective-permute-done.refs_0_.share_ref), custom_call_target="tpu_custom_call" | custom-call | flops 1000000000 | tf_op jit(solution)/shard_map/near/pallas_call | solution.py:256
  22.5 0.0 copy-start
  22.5 0.0 copy-start.8
  22.6 0.0 collective-permute-done.4.first_ref
  22.6 0.0 collective-permute-done.5.second_ref
  22.6 0.0 collective-permute-done.6.third_ref
  22.6 0.1 column.1
  22.6 3.6 %collective-permute-start.7 = (bf16[1024,256]{1,0:T(8,128)(2,1)S(1)}, bf16[1024,256]{1,0:T(8,128)(2,1)S(1)}, u32[]{:S(2)}, u32[]{:S(2)}) collective-permute-start(bf16[1024,256]{1,0:T(8,128)(2,1)S(1)} %get-tuple-element.7.column_ref), channel_id=1, source_target_pairs={{0,1},{1,0},{2,3},{3,2},{4,5},{5,4},{6,7},{7,6},{8,9},{9,8},{10,11... | collective-permute-start | bytes 1572872 | tf_op jit(solution)/shard_map/ppermute | solution.py:289
  26.2 0.0 collective-permute-start.9
  26.2 0.0 collective-permute-done.3.layer_ref
  26.3 0.0 copy-start.4
  26.3 0.0 copy-start.5
  26.3 0.0 copy-start.6
  26.3 0.0 copy-start.9
  26.3 0.2 collective-permute-start.8
  26.5 0.0 collective-permute-done.1.across_ref
  26.5 4.1 %across.1.refs_0_.near_ref = f32[4,256,256]{2,1,0:T(8,128)S(1)} custom-call(s32[4,16]{1,0:T(4,128)S(1)} %fusion.4.index_ref, bf16[4,16,256,256]{3,2,1,0:T(8,128)(2,1)} %blocks_hbm.3, f32[4,256,256]{2,1,0:T(8,128)S(1)} %near.1.near_ref._, bf16[1024,256]{1,0:T(8,128)(2,1)S(1)} %collective-permute-done.1.across_ref), custom_call_target="tpu_custom_call" | custom-call | tf_op jit(solution)/shard_map/across/pallas_call | solution.py:256
  30.6 2.1 %collective-permute-done.9.in_ref = bf16[384,256]{1,0:T(8,128)(2,1)S(1)} collective-permute-done((bf16[384,256]{1,0:T(8,128)(2,1)S(1)}, bf16[384,256]{1,0:T(8,128)(2,1)S(1)}, u32[]{:S(2)}, u32[]{:S(2)}) %collective-permute-start.9) | collective-permute-done | bytes 196640 | tf_op jit(solution)/shard_map/ppermute | solution.py:289
  32.7 0.9 %collective-permute-start.10 = (bf16[384,256]{1,0:T(8,128)(2,1)S(1)}, bf16[384,256]{1,0:T(8,128)(2,1)S(1)}, u32[]{:S(2)}, u32[]{:S(2)}) collective-permute-start(bf16[384,256]{1,0:T(8,128)(2,1)S(1)} %hand.1.beside_ref), channel_id=1, source_target_pairs={{0,1},{1,0},{2,3},{3,2},{4,5},{5,4},{6,7},{7,6},{8,9},{9,8},{10,11... | collective-permute-start | bytes 589832 | tf_op jit(solution)/shard_map/ppermute | solution.py:289
  33.6 0.0 collective-permute-done.8.passed_ref
  33.6 0.0 collective-permute-done.7.share_ref.their_column_ref
  33.6 0.0 copy-done
  33.7 0.0 copy-done.8
  33.7 1.5 %far.1.far_ref = f32[512,256]{1,0:T(8,128)S(1)} custom-call(s32[4,16]{1,0:T(4,128)S(1)} %copy-done.8, bf16[4,16,128,128]{3,2,1,0:T(8,128)(2,1)S(1)} %copy-done, bf16[512,256]{1,0:T(8,128)(2,1)S(1)} %collective-permute-done.2.level_ref, bf16[512,256]{1,0:T(8,128)(2,1)S(1)} %collective-permute-done.3.layer_ref, ...), custom_call_target="tpu_custom_call" | custom-call | flops 536870912 | bytes 2097152 | tf_op jit(solution)/shard_map/far/pallas_call | solution.py:256
  35.1 0.0 collective-permute-done.10.their_beside_ref
  35.2 0.0 copy-done.4
  35.2 0.0 copy-done.5
  35.2 0.0 copy-done.6
  35.2 0.0 copy-done.9
  35.2 2.1 %down.1 = bf16[1024,256]{1,0:T(8,128)(2,1)} custom-call(s32[1,8]{1,0:T(1,128)S(1)} %copy-done.9, bf16[4,128,128]{2,1,0:T(8,128)(2,1)S(1)} %copy-done.4, bf16[1,8,128,128]{3,2,1,0:T(8,128)(2,1)S(1)} %copy-done.5, bf16[4,256,128]{2,1,0:T(8,128)(2,1)S(1)} %copy-done.6, f32[4,256,256]{2,1,0:T(8,128)S(1)} %across.1.refs_0_.near_ref, f32[512,256]{1,0:T(8,128)S(1)} %far.1.far_ref, ...), custom_call_target="tpu_custom_call" | custom-call | flops 134217728 | bytes 1048576 | tf_op jit(solution)/shard_map/down/pallas_call | solution.py:256
  (3 shorter events, 0.1 us)
Async XLA Ops:
  0.0 9.9 %collective-permute-start = (bf16[1024,256]{1,0:T(8,128)(2,1)}, bf16[1024,256]{1,0:T(8,128)(2,1)S(1)}, u32[]{:S(2)}, u32[]{:S(2)}) collective-permute-start(bf16[1024,256]{1,0:T(8,128)(2,1)} %source_ref.1), channel_id=1, source_target_pairs={{0,1},{1,0},{2,3},{3,2},{4,5},{5,4},{6,7},{7,6},{8,9},{9,8},{10,11... | collective-permute-start | bytes 1572872 | tf_op jit(solution)/shard_map/ppermute | solution.py:289
  0.1 1.0 %copy-start.1 = (bf16[1024,256]{1,0:T(8,128)(2,1)S(1)}, bf16[1024,256]{1,0:T(8,128)(2,1)}, u32[]{:S(2)}) copy-start(bf16[1024,256]{1,0:T(8,128)(2,1)} %source_ref.1) | copy-start | bytes 1572868
  1.1 0.9 %copy-start.7 = (bf16[4,256,128]{2,1,0:T(8,128)(2,1)S(1)}, bf16[4,256,128]{2,1,0:T(8,128)(2,1)}, u32[]{:S(2)}) copy-start(bf16[4,256,128]{2,1,0:T(8,128)(2,1)} %col_ref.1) | copy-start | bytes 786436
  2.3 12.3 %collective-permute-start.2 = (bf16[512,256]{1,0:T(8,128)(2,1)S(1)}, bf16[512,256]{1,0:T(8,128)(2,1)S(1)}, u32[]{:S(2)}, u32[]{:S(2)}) collective-permute-start(bf16[512,256]{1,0:T(8,128)(2,1)S(1)} %coef.1.coef_ref), channel_id=1, source_target_pairs={{0,2},{1,3},{2,0},{3,1},{4,6},{5,7},{6,4},{7,5},{8,10},{9,11},{10,... | collective-permute-start | bytes 786440 | tf_op jit(solution)/shard_map/ppermute | solution.py:289
  5.1 0.9 %copy-start.3 = (bf16[4,128,128]{2,1,0:T(8,128)(2,1)S(1)}, bf16[4,128,128]{2,1,0:T(8,128)(2,1)}, u32[]{:S(2)}) copy-start(bf16[4,128,128]{2,1,0:T(8,128)(2,1)} %transfer_ref.3) | copy-start | bytes 393220
  6.2 16.3 %collective-permute-start.4 = (bf16[128,256]{1,0:T(8,128)(2,1)S(1)}, bf16[128,256]{1,0:T(8,128)(2,1)S(1)}, u32[]{:S(2)}, u32[]{:S(2)}) collective-permute-start(bf16[128,256]{1,0:T(8,128)(2,1)S(1)} %parent.1.own_ref), channel_id=1, source_target_pairs={{0,4},{1,5},{2,6},{3,7},{4,0},{5,1},{6,2},{7,3},{8,12},{9,13},{10,... | collective-permute-start | bytes 196616 | tf_op jit(solution)/shard_map/ppermute | solution.py:289
  7.6 15.0 %collective-permute-start.5 = (bf16[128,256]{1,0:T(8,128)(2,1)S(1)}, bf16[128,256]{1,0:T(8,128)(2,1)S(1)}, u32[]{:S(2)}, u32[]{:S(2)}) collective-permute-start(bf16[128,256]{1,0:T(8,128)(2,1)S(1)} %parent.1.own_ref), channel_id=1, source_target_pairs={{0,8},{1,9},{2,10},{3,11},{4,12},{5,13},{6,14},{7,15},{8,0},{9,1},... | collective-permute-start | bytes 196616 | tf_op jit(solution)/shard_map/ppermute | solution.py:289
  9.9 12.7 %collective-permute-start.6 = (bf16[128,256]{1,0:T(8,128)(2,1)S(1)}, bf16[128,256]{1,0:T(8,128)(2,1)S(1)}, u32[]{:S(2)}, u32[]{:S(2)}) collective-permute-start(bf16[128,256]{1,0:T(8,128)(2,1)S(1)} %parent.1.own_ref), channel_id=1, source_target_pairs={{0,12},{1,13},{2,14},{3,15},{4,8},{5,9},{6,10},{7,11},{8,4},{9,5},... | collective-permute-start | bytes 196616 | tf_op jit(solution)/shard_map/ppermute | solution.py:289
  9.9 1.0 %copy-start.2 = (bf16[1024,256]{1,0:T(8,128)(2,1)S(1)}, bf16[1024,256]{1,0:T(8,128)(2,1)}, u32[]{:S(2)}) copy-start(bf16[1024,256]{1,0:T(8,128)(2,1)} %source_ref.1) | copy-start | bytes 1572868
  11.0 15.5 %collective-permute-start.1 = (bf16[1024,256]{1,0:T(8,128)(2,1)S(1)}, bf16[1024,256]{1,0:T(8,128)(2,1)S(1)}, u32[]{:S(2)}, u32[]{:S(2)}) collective-permute-start(bf16[1024,256]{1,0:T(8,128)(2,1)S(1)} %panels.1.own_ref), channel_id=1, source_target_pairs={{1,2},{2,1},{3,4},{4,3},{5,6},{6,5},{7,8},{8,7},{9,10},{10,9},{11,... | collective-permute-start | bytes 1572872 | tf_op jit(solution)/shard_map/ppermute | solution.py:289
  14.6 11.6 %collective-permute-start.3 = (bf16[512,256]{1,0:T(8,128)(2,1)S(1)}, bf16[512,256]{1,0:T(8,128)(2,1)S(1)}, u32[]{:S(2)}, u32[]{:S(2)}) collective-permute-start(bf16[512,256]{1,0:T(8,128)(2,1)S(1)} %collective-permute-done.2.level_ref), channel_id=1, source_target_pairs={{0,4},{1,5},{4,8},{5,9},{6,2},{7,3},{8,12},{9,13},{10,6},{11,7},{1... | collective-permute-start | bytes 786440 | tf_op jit(solution)/shard_map/ppermute | solution.py:289
  22.5 11.1 %copy-start = (bf16[4,16,128,128]{3,2,1,0:T(8,128)(2,1)S(1)}, bf16[4,16,128,128]{3,2,1,0:T(8,128)(2,1)}, u32[]{:S(2)}) copy-start(bf16[4,16,128,128]{3,2,1,0:T(8,128)(2,1)} %coupling_ref.2) | copy-start | bytes 6291460
  22.5 11.1 %copy-start.8 = (s32[4,16]{1,0:T(4,128)S(1)}, s32[4,16]{1,0:T(4,128)}, u32[]{:S(2)}) copy-start(s32[4,16]{1,0:T(4,128)} %list_ref.2) | copy-start | bytes 772
  22.6 11.0 %collective-permute-start.7 = (bf16[1024,256]{1,0:T(8,128)(2,1)S(1)}, bf16[1024,256]{1,0:T(8,128)(2,1)S(1)}, u32[]{:S(2)}, u32[]{:S(2)}) collective-permute-start(bf16[1024,256]{1,0:T(8,128)(2,1)S(1)} %get-tuple-element.7.column_ref), channel_id=1, source_target_pairs={{0,1},{1,0},{2,3},{3,2},{4,5},{5,4},{6,7},{7,6},{8,9},{9,8},{10,11... | collective-permute-start | bytes 1572872 | tf_op jit(solution)/shard_map/ppermute | solution.py:289
  26.2 6.5 %collective-permute-start.9 = (bf16[384,256]{1,0:T(8,128)(2,1)S(1)}, bf16[384,256]{1,0:T(8,128)(2,1)S(1)}, u32[]{:S(2)}, u32[]{:S(2)}) collective-permute-start(bf16[384,256]{1,0:T(8,128)(2,1)S(1)} %get-tuple-element.8), channel_id=1, source_target_pairs={{0,2},{1,3},{2,0},{3,1},{4,6},{5,7},{6,4},{7,5},{8,10},{9,11},{10,... | collective-permute-start | bytes 589832 | tf_op jit(solution)/shard_map/ppermute | solution.py:289
  26.3 8.9 %copy-start.4 = (bf16[4,128,128]{2,1,0:T(8,128)(2,1)S(1)}, bf16[4,128,128]{2,1,0:T(8,128)(2,1)}, u32[]{:S(2)}) copy-start(bf16[4,128,128]{2,1,0:T(8,128)(2,1)} %transfer_ref.3) | copy-start | bytes 393220
  26.3 8.9 %copy-start.5 = (bf16[1,8,128,128]{3,2,1,0:T(8,128)(2,1)S(1)}, bf16[1,8,128,128]{3,2,1,0:T(8,128)(2,1)}, u32[]{:S(2)}) copy-start(bf16[1,8,128,128]{3,2,1,0:T(8,128)(2,1)} %coupling_ref.3) | copy-start | bytes 786436
  26.3 8.9 %copy-start.6 = (bf16[4,256,128]{2,1,0:T(8,128)(2,1)S(1)}, bf16[4,256,128]{2,1,0:T(8,128)(2,1)}, u32[]{:S(2)}) copy-start(bf16[4,256,128]{2,1,0:T(8,128)(2,1)} %row_ref.1) | copy-start | bytes 786436
  26.3 8.9 %copy-start.9 = (s32[1,8]{1,0:T(1,128)S(1)}, s32[1,8]{1,0:T(1,128)}, u32[]{:S(2)}) copy-start(s32[1,8]{1,0:T(1,128)} %list_ref.3) | copy-start | bytes 100
  26.3 7.3 %collective-permute-start.8 = (bf16[512,256]{1,0:T(8,128)(2,1)S(1)}, bf16[512,256]{1,0:T(8,128)(2,1)S(1)}, u32[]{:S(2)}, u32[]{:S(2)}) collective-permute-start(bf16[512,256]{1,0:T(8,128)(2,1)S(1)} %pick.1), channel_id=1, source_target_pairs={{0,1},{1,0},{2,3},{3,2},{4,5},{5,4},{6,7},{7,6},{8,9},{9,8},{10,11... | collective-permute-start | bytes 786440 | tf_op jit(solution)/shard_map/ppermute | solution.py:289
  32.7 2.4 %collective-permute-start.10 = (bf16[384,256]{1,0:T(8,128)(2,1)S(1)}, bf16[384,256]{1,0:T(8,128)(2,1)S(1)}, u32[]{:S(2)}, u32[]{:S(2)}) collective-permute-start(bf16[384,256]{1,0:T(8,128)(2,1)S(1)} %hand.1.beside_ref), channel_id=1, source_target_pairs={{0,1},{1,0},{2,3},{3,2},{4,5},{5,4},{6,7},{7,6},{8,9},{9,8},{10,11... | collective-permute-start | bytes 589832 | tf_op jit(solution)/shard_map/ppermute | solution.py:289
